TPU v7x, 128 devices: a whole 4x4x4 slice. The times are simulated.
128 devices in a mesh: row: 8 (over x, y_lo), col: 16 (over z, y_hi, core).
Axes of the slice: x: 4, y: 4 (y_hi: 2, y_lo: 2; y = y_hi * 2 + y_lo), z: 4, core: 2. Of those that a mesh axis runs over, the one named last changes fastest.
Arguments:
- input_a: bfloat16 [512, 12288], P('row', 'col'), may hold values from -6 to 6
- input_b: bfloat16 [512, 12288], P('row', 'col'), may hold values from -6 to 6
- cotangent: bfloat16 [512, 12288], P('row', 'col'), may hold values from -1.5 to 1.5
- weight_in: bfloat16 [12288, 24576], P('col', 'row'), may hold values from -0.0546875 to 0.0546875
- bias_in: float32 [24576], P('row'), may hold values from -3 to 3
- weight_out: bfloat16 [24576, 12288], P('row', 'col'), may hold values from -0.0390625 to 0.0390625
- bias_out: float32 [12288], P('col'), may hold values from -3 to 3
Outputs:
- output_a: bfloat16 [512, 12288], P('row', 'col')
- grad_input: bfloat16 [512, 12288], P('row', 'col')
- grad_weight_in: bfloat16 [12288, 24576], P('col', 'row')
- grad_bias_in: float32 [24576], P('row')
- grad_weight_out: bfloat16 [24576, 12288], P('row', 'col')
- grad_bias_out: float32 [12288], P('col')
All inputs are finite; a program needn't handle non-finite values.
Results may differ from a plain program's by a relative error of at most 0.007.
Values may be sent and summed in bfloat16 or wider, within the bound.
No kernel may reach another device: no remote copies, remote signals or barrier semaphores. Data moves between devices by JAX's collectives and lax.ppermute only.
A program may use at most 128 MiB of HBM per device.

v0:
```python
import jax
import jax.numpy as jnp
from jax import lax
from jax.sharding import PartitionSpec as P

coeff = 0.7978845608
outer = (((0,), (0,)), ((), ()))
inner = (((1,), (1,)), ((), ()))


def gelu_tanh(values):
    return 0.5 * values * (1.0 + jnp.tanh(coeff * (values + 0.044715 * values * values * values)))


def gelu_slope(values):
    tangent = jnp.tanh(coeff * (values + 0.044715 * values * values * values))
    return 0.5 * (1.0 + tangent) + 0.5 * values * (1.0 - tangent * tangent) * coeff * (
        1.0 + 3.0 * 0.044715 * values * values
    )


def per_device(input_a, input_b, cotangent, weight_in, bias_in, weight_out, bias_out):
    partial_a = jnp.dot(
        lax.all_gather(input_a, "row", axis=0, tiled=True),
        weight_in,
        preferred_element_type=jnp.float32,
    )
    pre_a = lax.psum_scatter(partial_a, "col", scatter_dimension=0, tiled=True) + bias_in
    hidden_a = gelu_tanh(pre_a).astype(jnp.bfloat16)
    out_terms = jnp.dot(
        lax.all_gather(hidden_a, "col", axis=0, tiled=True),
        weight_out,
        preferred_element_type=jnp.float32,
    )
    output_a = (
        lax.psum_scatter(out_terms, "row", scatter_dimension=0, tiled=True) + bias_out
    ).astype(jnp.bfloat16)
    full_input, full_cot = (
        lax.all_gather(input_b, "row", axis=0, tiled=True),
        lax.all_gather(cotangent, "row", axis=0, tiled=True),
    )
    partial_b = jnp.dot(full_input, weight_in, preferred_element_type=jnp.float32)
    grad_bias_out = jnp.sum(full_cot.astype(jnp.float32), axis=0)
    pre_b = lax.psum_scatter(partial_b, "col", scatter_dimension=0, tiled=True) + bias_in
    hidden_b = gelu_tanh(pre_b).astype(jnp.bfloat16)
    cot_rows = full_cot
    grad_weight_out = lax.dot_general(
        lax.all_gather(hidden_b, "col", axis=0, tiled=True),
        cot_rows,
        outer,
        preferred_element_type=jnp.float32,
    ).astype(jnp.bfloat16)
    cot_rows = full_cot
    back_hidden = lax.psum_scatter(
        lax.dot_general(cot_rows, weight_out, inner, preferred_element_type=jnp.float32),
        "col",
        scatter_dimension=0,
        tiled=True,
    )
    back_pre = (back_hidden * gelu_slope(pre_b)).astype(jnp.bfloat16)
    grad_bias_in = lax.psum(jnp.sum(back_pre.astype(jnp.float32), axis=0), "col")
    full_back = lax.all_gather(back_pre, "col", axis=0, tiled=True)
    grad_weight_in = lax.dot_general(
        full_input, full_back, outer, preferred_element_type=jnp.float32
    ).astype(jnp.bfloat16)
    grad_input = lax.psum_scatter(
        lax.dot_general(full_back, weight_in, inner, preferred_element_type=jnp.float32),
        "row",
        scatter_dimension=0,
        tiled=True,
    ).astype(jnp.bfloat16)
    return (output_a, grad_input, grad_weight_in, grad_bias_in, grad_weight_out, grad_bias_out)


def solution(mesh):
    return jax.shard_map(
        per_device,
        mesh=mesh,
        in_specs=(
            P("row", "col"),
            P("row", "col"),
            P("row", "col"),
            P("col", "row"),
            P("row"),
            P("row", "col"),
            P("col"),
        ),
        out_specs=(
            P("row", "col"),
            P("row", "col"),
            P("col", "row"),
            P("row"),
            P("row", "col"),
            P("col"),
        ),
        check_vma=False,
    )
```

profile of v0, /device:TPU:0, one launch (start us, length us, event | category | flops | bytes accessed | tf_op | source)
XLA Modules:
  0.0 590.7 jit_solution(17069214509920193509)
XLA Ops:
  7.2 0.0 reduce-scatter.10.cloned.1.call-start
  7.2 30.2 %all_gather.20 = bf16[512,768]{1,0:T(8,128)(2,1)S(1)} all-gather(bf16[64,768]{1,0:T(8,128)(2,1)} %param.9), channel_id=1, replica_groups=mesh['row'=8,'col'=16] {'row'}, dimensions={0}, use_global_device_ids=true | all-gather | bytes 884736 | tf_op jit(solution)/shard_map/all_gather | solution.py:40
  37.4 6.9 %fusion.16 = f32[512,3072]{1,0:T(8,128)} fusion(bf16[512,768]{1,0:T(8,128)(2,1)S(1)} %all_gather.20, bf16[3072,768]{1,0:T(8,128)(2,1)} %param.12), kind=kOutput, calls=%fused_computation.24 | convolution fusion | flops 2415919104 | bytes 11796480 | tf_op jit(solution)/shard_map/dot_general | solution.py:55
  44.3 0.0 copy-start
  44.3 0.0 reduce-scatter.10.cloned.1.call-update
  44.3 0.0 reduce-scatter.12.cloned.1.call-start
  44.4 0.8 copy-done
  45.2 29.3 %all_gather.21 = bf16[512,768]{1,0:T(8,128)(2,1)S(1)} all-gather(bf16[64,768]{1,0:T(8,128)(2,1)S(1)} %copy-done), channel_id=1, replica_groups=mesh['row'=8,'col'=16] {'row'}, dimensions={0}, use_global_device_ids=true | all-gather | bytes 884736 | tf_op jit(solution)/shard_map/all_gather | solution.py:39
  74.5 6.8 %fusion.17 = f32[512,3072]{1,0:T(8,128)} fusion(bf16[512,768]{1,0:T(8,128)(2,1)S(1)} %all_gather.21, bf16[768,3072]{1,0:T(8,128)(2,1)} %param.10), kind=kOutput, calls=%fused_computation.25 | convolution fusion | flops 2415919104 | bytes 11796480 | tf_op jit(solution)/shard_map/dot_general | solution.py:42
  81.3 0.0 copy-start.1
  81.3 0.0 reduce-scatter.12.cloned.1.call-update
  81.3 0.0 reduce-scatter.6.cloned.1.call-start
  81.3 0.9 copy-done.1
  82.2 31.8 %all_gather.18 = bf16[512,768]{1,0:T(8,128)(2,1)S(1)} all-gather(bf16[64,768]{1,0:T(8,128)(2,1)S(1)} %copy-done.1), channel_id=1, replica_groups=mesh['row'=8,'col'=16] {'row'}, dimensions={0}, use_global_device_ids=true | all-gather | bytes 884736 | tf_op jit(solution)/shard_map/all_gather | solution.py:24
  114.0 7.1 %fusion.14 = f32[512,3072]{1,0:T(8,128)} fusion(bf16[512,768]{1,0:T(8,128)(2,1)S(1)} %all_gather.18, bf16[768,3072]{1,0:T(8,128)(2,1)} %param.10), kind=kOutput, calls=%fused_computation.22 | convolution fusion | flops 2415919104 | bytes 11796480 | tf_op jit(solution)/shard_map/dot_general | solution.py:23
  121.1 0.0 copy-start.2
  121.1 0.0 reduce-scatter.6.cloned.1.call-update
  121.1 0.0 all-gather.6.cloned.1.call-start
  121.2 25.1 %reduce-scatter.10.cloned.1.call-done = f32[32,3072]{1,0:T(8,128)} async-done(((f32[512,3072]{1,0:T(8,128)}), f32[32,3072]{1,0:T(8,128)}) %reduce-scatter.10.cloned.1.call-update) | async-done | bytes 393232 | tf_op jit(solution)/shard_map/reduce_scatter | solution.py:54
  146.2 93.4 %reduce-scatter.12.cloned.1.call-done = f32[32,3072]{1,0:T(8,128)} async-done(((f32[512,3072]{1,0:T(8,128)}), f32[32,3072]{1,0:T(8,128)}) %reduce-scatter.12.cloned.1.call-update) | async-done | bytes 393232 | tf_op jit(solution)/shard_map/reduce_scatter | solution.py:44
  239.6 92.8 %reduce-scatter.6.cloned.1.call-done = f32[32,3072]{1,0:T(8,128)} async-done(((f32[512,3072]{1,0:T(8,128)}), f32[32,3072]{1,0:T(8,128)}) %reduce-scatter.6.cloned.1.call-update) | async-done | bytes 393232 | tf_op jit(solution)/shard_map/reduce_scatter | solution.py:28
  332.4 0.0 copy-done.2
  332.4 2.4 convert_reduce_fusion.1
  334.9 0.0 all-gather.6.cloned.1.call-update
  334.9 0.0 all-gather.4.cloned.1.call-start
  334.9 0.5 all-gather.4.cloned.1.call-update
  335.5 0.0 all-gather.8.cloned.1.call-start
  335.5 0.5 all-gather.8.cloned.1.call-update
  336.1 0.0 reduce-scatter.14.cloned.1.call-start
  336.1 49.1 %all-gather.6.cloned.1.call-done = bf16[512,3072]{1,0:T(8,128)(2,1)} async-done(((bf16[32,3072]{1,0:T(8,128)(2,1)}), bf16[512,3072]{1,0:T(8,128)(2,1)}) %all-gather.6.cloned.1.call-update) | async-done | bytes 3145744 | tf_op jit(solution)/shard_map/all_gather | solution.py:62
  385.2 7.1 %fusion.18 = f32[512,768]{1,0:T(8,128)} fusion(bf16[512,3072]{1,0:T(8,128)(2,1)} %all-gather.6.cloned.1.call-done, bf16[768,3072]{1,0:T(8,128)(2,1)} %param.10), kind=kOutput, calls=%fused_computation.26 | convolution fusion | flops 2415919104 | bytes 9437184 | tf_op jit(solution)/shard_map/dot_general | solution.py:67
  392.3 0.0 reduce-scatter.14.cloned.1.call-update
  392.4 0.0 reduce-scatter.8.cloned.1.call-start
  392.4 45.6 %all-gather.4.cloned.1.call-done = bf16[512,3072]{1,0:T(8,128)(2,1)} async-done(((bf16[32,3072]{1,0:T(8,128)(2,1)}), bf16[512,3072]{1,0:T(8,128)(2,1)}) %all-gather.4.cloned.1.call-update) | async-done | bytes 3145744 | tf_op jit(solution)/shard_map/all_gather | solution.py:31
  438.0 7.0 %fusion.15 = f32[512,768]{1,0:T(8,128)} fusion(bf16[512,3072]{1,0:T(8,128)(2,1)} %all-gather.4.cloned.1.call-done, bf16[3072,768]{1,0:T(8,128)(2,1)} %param.12), kind=kOutput, calls=%fused_computation.23 | convolution fusion | flops 2415919104 | bytes 9437184 | tf_op jit(solution)/shard_map/dot_general | solution.py:30
  445.1 0.0 reduce-scatter.8.cloned.1.call-update
  445.1 0.7 convert_reduce_fusion
  445.8 67.6 %psum.7 = f32[3072]{0:T(1024)} all-reduce(f32[3072]{0:T(1024)S(1)} %get-tuple-element.12), channel_id=1, replica_groups=mesh['row'=8,'col'=16] {'col'}, use_global_device_ids=true, to_apply=%region_6.0 | all-reduce | flops 3072 | bytes 24576 | tf_op jit(solution)/shard_map/psum | solution.py:61
  513.4 6.7 %fusion = bf16[768,3072]{0,1:T(8,128)(2,1)} fusion(bf16[512,3072]{1,0:T(8,128)(2,1)} %all-gather.6.cloned.1.call-done, bf16[512,768]{1,0:T(8,128)(2,1)S(1)} %all_gather.21), kind=kOutput, calls=%fused_computation.2 | convolution fusion | flops 2418278400 | bytes 8650752 | tf_op jit(solution)/shard_map/dot_general | solution.py:63
  520.1 6.6 %copy.13 = bf16[768,3072]{1,0:T(8,128)(2,1)} copy(bf16[768,3072]{0,1:T(8,128)(2,1)} %fusion) | data formatting | bytes 9437184
  526.7 0.0 copy-start.3
  526.8 0.0 all-gather.8.cloned.1.call-done
  526.8 6.8 %convolution_convert_fusion = bf16[3072,768]{1,0:T(8,128)(2,1)} fusion(bf16[512,3072]{1,0:T(8,128)(2,1)} %all-gather.8.cloned.1.call-done, bf16[512,768]{1,0:T(8,128)(2,1)S(1)} %all_gather.20), kind=kOutput, calls=%fused_computation | convolution fusion | flops 2418278400 | bytes 8650752 | tf_op jit(solution)/shard_map/dot_general | solution.py:47
  533.5 2.7 reduce-scatter.14.cloned.1.call-done
  536.2 1.6 convert_element_type.33
  537.8 44.5 %reduce-scatter.8.cloned.1.call-done = f32[64,768]{1,0:T(8,128)} async-done(((f32[512,768]{1,0:T(8,128)}), f32[64,768]{1,0:T(8,128)}) %reduce-scatter.8.cloned.1.call-update) | async-done | bytes 196624 | tf_op jit(solution)/shard_map/reduce_scatter | solution.py:36
  582.3 0.0 copy-done.3
  582.3 1.6 add_convert_fusion
Async XLA Ops:
  7.2 139.1 %reduce-scatter.10.cloned.1.call-start = ((), (), s32[]{:S(2)}) async-start(), calls=%async_computation.8 | async-start | bytes 6684672 | tf_op jit(solution)/shard_map/reduce_scatter | solution.py:54
  44.3 0.9 copy-start
  44.3 195.3 %reduce-scatter.12.cloned.1.call-start = ((), (), s32[]{:S(2)}) async-start(), calls=%async_computation.9 | async-start | bytes 6684672 | tf_op jit(solution)/shard_map/reduce_scatter | solution.py:44
  81.3 0.9 copy-start.1
  81.3 251.1 %reduce-scatter.6.cloned.1.call-start = ((), (), s32[]{:S(2)}) async-start(), calls=%async_computation.5 | async-start | bytes 6684672 | tf_op jit(solution)/shard_map/reduce_scatter | solution.py:28
  121.1 211.3 %copy-start.2 = (f32[3072]{0:T(1024)S(1)}, f32[3072]{0:T(1024)}, u32[]{:S(2)}) copy-start(f32[3072]{0:T(1024)} %param.11) | copy-start | bytes 36868
  121.1 264.1 %all-gather.6.cloned.1.call-start = ((), (), s32[]{:S(2)}) async-start(), calls=%async_computation.10 | async-start | bytes 3342336 | tf_op jit(solution)/shard_map/all_gather | solution.py:62
  334.9 103.1 %all-gather.4.cloned.1.call-start = ((), (), s32[]{:S(2)}) async-start(), calls=%async_computation.6 | async-start | bytes 3342336 | tf_op jit(solution)/shard_map/all_gather | solution.py:31
  335.5 191.3 %all-gather.8.cloned.1.call-start = ((), (), s32[]{:S(2)}) async-start(), calls=%async_computation.12 | async-start | bytes 3342336 | tf_op jit(solution)/shard_map/all_gather | solution.py:48
  336.1 200.1 %reduce-scatter.14.cloned.1.call-start = ((), (), s32[]{:S(2)}) async-start(), calls=%async_computation.11 | async-start | bytes 1769472 | tf_op jit(solution)/shard_map/reduce_scatter | solution.py:66
  392.4 189.9 %reduce-scatter.8.cloned.1.call-start = ((), (), s32[]{:S(2)}) async-start(), calls=%async_computation.7 | async-start | bytes 1769472 | tf_op jit(solution)/shard_map/reduce_scatter | solution.py:36
  526.7 55.5 %copy-start.3 = (f32[768]{0:T(1024)S(1)}, f32[768]{0:T(1024)}, u32[]{:S(2)}) copy-start(f32[768]{0:T(1024)} %param.13) | copy-start | bytes 9220
Sparse Core Ops, SparseCore 0:
  44.4 101.7 reduce-scatter.9
  151.0 88.5 reduce-scatter.11
  243.8 88.5 reduce-scatter.5
  335.6 49.5 all-gather.5
  388.4 49.5 all-gather.3
  440.6 49.8 all-gather.7
  493.0 43.1 reduce-scatter.13
  538.7 43.4 reduce-scatter.7
where the time goes:
time: 591 us
  waiting for transfers between devices  354 us (60%)
  blocking collectives  159 us (27%)
  matrix products  48.4 us (8%)
  between operations  14.1 us (2%)
  local copies, waits for them, and re-layouts  8.32 us (1%)
  other arithmetic  6.34 us (1%)
    reduce_scatter x1, waiting for transfers between devices, per_device(): lax.psum_scatter(partial_b, 'col', scatter_dimension=0, tiled=True)  93.4 us
    reduce_scatter x1, waiting for transfers between devices, per_device(): lax.psum_scatter(partial_a, 'col', scatter_dimension=0, tiled=True)  92.8 us
    psum x1, blocking collectives, per_device(): lax.psum(jnp.sum(back_pre.astype(jnp.float32), axis=0), 'col')  67.6 us
    all_gather x1, waiting for transfers between devices, per_device(): full_back = lax.all_gather(back_pre, 'col', axis=0, tiled=True)  49.1 us
    all_gather x1, waiting for transfers between devices, per_device(): lax.all_gather(hidden_a, 'col', axis=0, tiled=True)  45.6 us
    reduce_scatter x1, waiting for transfers between devices, per_device(): lax.psum_scatter(out_terms, 'row', scatter_dimension=0, tiled=True)  44.5 us
    all_gather x1, blocking collectives, per_device(): lax.all_gather(input_a, 'row', axis=0, tiled=True)  31.8 us
    all_gather x1, blocking collectives, per_device(): lax.all_gather(cotangent, 'row', axis=0, tiled=True)  30.2 us
  transfers between devices with their start and end apart: 8, of which 7 were waited for; matrix products, arithmetic and copies ran while one was open for 9% of the time, Pallas kernels for 0%

commit v1 on v0

v1 whole, which is shorter than its diff:
```python
import jax
import jax.numpy as jnp
from jax import lax
from jax.sharding import Mesh, PartitionSpec as P

coeff = 0.7978845608
outer = (((0,), (0,)), ((), ()))
inner = (((1,), (1,)), ((), ()))
ROW = ("x", "yl")
CHIPS = ("z", "yh")
COL = ("z", "yh", "core")
f32 = jnp.float32
bf16 = jnp.bfloat16


def gelu_tanh(values):
    return 0.5 * values * (1.0 + jnp.tanh(coeff * (values + 0.044715 * values * values * values)))


def gelu_slope(values):
    tangent = jnp.tanh(coeff * (values + 0.044715 * values * values * values))
    return 0.5 * (1.0 + tangent) + 0.5 * values * (1.0 - tangent * tangent) * coeff * (
        1.0 + 3.0 * 0.044715 * values * values
    )


def swap(values):
    return lax.ppermute(values, "core", [(0, 1), (1, 0)])


def spread(values, axes):
    members = lax.axis_size(axes)
    return lax.all_to_all(jnp.broadcast_to(values, (members,) + values.shape), axes, 0, 0)


def collect(parts, axes):
    return jnp.sum(lax.all_to_all(parts, axes, 0, 0).astype(f32), axis=0)


def tokens_of(values):
    count, width = values.shape
    half = count // 2
    core = lax.axis_index("core")
    mine = lax.dynamic_slice(values, (core * half, 0), (half, width))
    other = lax.dynamic_slice(values, ((1 - core) * half, 0), (half, width))
    rows = spread(jnp.concatenate([mine, other], 0), ROW)
    return rows[:, :half].reshape(-1, width), rows[:, half:].reshape(-1, width)


def sum_features(pair, weight, dims):
    mine, other = pair
    sent = swap(lax.dot_general(other, weight, dims, preferred_element_type=f32).astype(bf16))
    kept = lax.dot_general(mine, weight, dims, preferred_element_type=f32)
    both = (kept + sent.astype(f32)).astype(bf16)
    chips = lax.axis_size(CHIPS)
    return collect(both.reshape(chips, both.shape[0] // chips, both.shape[1]), CHIPS)


def all_tokens(values):
    mine = spread(values, CHIPS).reshape(-1, values.shape[1])
    return mine, swap(mine)


def sum_hidden(mine, other):
    rows = lax.axis_size(ROW)
    width = mine.shape[1]
    half = mine.shape[0] // rows
    parts = jnp.concatenate([mine.reshape(rows, half, width), other.reshape(rows, half, width)], 1)
    total = collect(parts, ROW)
    core = lax.axis_index("core")
    return lax.dynamic_slice(jnp.concatenate([total, total[:half]], 0), (core * half, 0), (2 * half, width))


plain = (((1,), (0,)), ((), ()))


def per_device(input_a, input_b, cotangent, weight_in, bias_in, weight_out, bias_out):
    rows_b = tokens_of(input_b)
    rows_cot = tokens_of(cotangent)
    rows_a = tokens_of(input_a)
    pre_b = sum_features(rows_b, weight_in, plain) + bias_in
    back_hidden = sum_features(rows_cot, weight_out, inner)
    pre_a = sum_features(rows_a, weight_in, plain) + bias_in
    back_pre = (back_hidden * gelu_slope(pre_b)).astype(bf16)
    hidden_b = gelu_tanh(pre_b).astype(bf16)
    hidden_a = gelu_tanh(pre_a).astype(bf16)

    full_back = all_tokens(back_pre)
    full_a = all_tokens(hidden_a)
    full_b = all_tokens(hidden_b)

    def both(pair):
        return jnp.concatenate(pair, 0)

    grad_input = sum_hidden(
        *[lax.dot_general(v, weight_in, inner, preferred_element_type=f32).astype(bf16) for v in full_back]
    ).astype(bf16)
    output_a = (
        sum_hidden(
            *[lax.dot_general(v, weight_out, plain, preferred_element_type=f32).astype(bf16) for v in full_a]
        )
        + bias_out
    ).astype(bf16)
    all_back = both(full_back)
    all_cot = both(rows_cot)
    grad_weight_in = lax.dot_general(
        both(rows_b), all_back, outer, preferred_element_type=f32
    ).astype(bf16)
    grad_bias_in = jnp.sum(all_back.astype(f32), axis=0)
    grad_weight_out = lax.dot_general(
        both(full_b), all_cot, outer, preferred_element_type=f32
    ).astype(bf16)
    grad_bias_out = jnp.sum(all_cot.astype(f32), axis=0)
    return (output_a, grad_input, grad_weight_in, grad_bias_in, grad_weight_out, grad_bias_out)


def solution(mesh):
    fine = Mesh(mesh.devices.reshape(4, 2, 4, 2, 2), ("x", "yl", "z", "yh", "core"))
    return jax.shard_map(
        per_device,
        mesh=fine,
        in_specs=(
            P(ROW, COL),
            P(ROW, COL),
            P(ROW, COL),
            P(COL, ROW),
            P(ROW),
            P(ROW, COL),
            P(COL),
        ),
        out_specs=(
            P(ROW, COL),
            P(ROW, COL),
            P(COL, ROW),
            P(ROW),
            P(ROW, COL),
            P(COL),
        ),
        check_vma=False,
    )
```

time: 591 us -> 267 us (0.45)
  waiting for transfers between devices: 354 us -> 100 us
  blocking collectives: 159 us -> 49.1 us
  starting transfers between devices: 0.32 us -> 40 us
  between operations: 14.1 us -> 1.02 us
  matrix products: 48.4 us -> 58.2 us
    reduce_scatter x5 -> x0, waiting for transfers between devices: 258 us -> none  [the longest x1 93.4 us: per_device(): lax.psum_scatter(partial_b, 'col', scatter_dimension=0, tiled=True)]
    all_to_all x0 -> x9, waiting for transfers between devices: none -> 100 us  [the longest x5 54.4 us: collect(): return jnp.sum(lax.all_to_all(parts, axes, 0, 0).astype(f32), axis=0)]
    all_gather x3 -> x0, waiting for transfers between devices: 94.7 us -> none  [the longest x1 49.1 us: per_device(): full_back = lax.all_gather(back_pre, 'col', axis=0, tiled=True)]
    all_gather x3 -> x0, blocking collectives: 91.3 us -> none  [the longest x1 31.8 us: per_device(): lax.all_gather(input_a, 'row', axis=0, tiled=True)]
    psum x1 -> x0, blocking collectives: 67.6 us -> none  [per_device(): lax.psum(jnp.sum(back_pre.astype(jnp.float32), axis=0), 'col')]
    all_to_all x0 -> x2, blocking collectives: none -> 49.1 us  [spread(): lax.all_to_all(jnp.broadcast_to(values, (members,) + values.shape), axes,...]
    all_to_all x0 -> x9, starting transfers between devices: none -> 39.4 us  [the longest x5 22.6 us: collect(): return jnp.sum(lax.all_to_all(parts, axes, 0, 0).astype(f32), axis=0)]
    dot_general x7 -> x12, matrix products: 48.4 us -> 58.2 us  [the longest x3 15.7 us: sum_features(): lax.dot_general(other, weight, dims, preferred_element_type=f32)]
  transfers between devices with their start and end apart: 8 -> 15, of which waited for: 7 -> 9; matrix products, arithmetic and copies ran while one was open for 9% -> 25% of each run, Pallas kernels for 0% -> 0%
where the time goes in v1:
time: 267 us; the launch traced here: 266 us
  waiting for transfers between devices  100 us (37%)
  matrix products  58.2 us (22%)
  blocking collectives  49.1 us (18%)
  starting transfers between devices  40 us (15%)
  other arithmetic  11.2 us (4%)
  local copies, waits for them, and re-layouts  6.37 us (2%)
    all_to_all x5, waiting for transfers between devices, collect(): return jnp.sum(lax.all_to_all(parts, axes, 0, 0).astype(f32), axis=0)  54.4 us
    all_to_all x2, blocking collectives, spread(): lax.all_to_all(jnp.broadcast_to(values, (members,) + values.shape), axes,...  49.1 us
    all_to_all x4, waiting for transfers between devices, spread(): lax.all_to_all(jnp.broadcast_to(values, (members,) + values.shape), axes,...  45.6 us
    all_to_all x5, starting transfers between devices, collect(): return jnp.sum(lax.all_to_all(parts, axes, 0, 0).astype(f32), axis=0)  22.6 us
    all_to_all x4, starting transfers between devices, spread(): lax.all_to_all(jnp.broadcast_to(values, (members,) + values.shape), axes,...  16.8 us
    dot_general x3, matrix products, sum_features(): lax.dot_general(other, weight, dims, preferred_element_type=f32)  15.7 us
    dot_general x3, matrix products, sum_features(): kept = lax.dot_general(mine, weight, dims, preferred_element_type=f32)  14.9 us
    dot_general x2, matrix products, per_device(): lax.dot_general(v, weight_out, plain, preferred_element_type=f32)  8.06 us
  transfers between devices with their start and end apart: 15, of which 9 were waited for; matrix products, arithmetic and copies ran while one was open for 25% of the time, Pallas kernels for 0%

profile of v1, /device:TPU:0, one launch (start us, length us, event | category | flops | bytes accessed | tf_op | source)
XLA Modules:
  0.0 266.0 jit_solution(10354529345098356861)
XLA Ops:
  0.6 0.9 constant_dynamic-slice_fusion.1
  1.6 0.9 broadcast_in_dim.24
  2.5 5.4 %all-to-all-start.6 = ((bf16[8,64,768]{2,1,0:T(8,128)(2,1)}), bf16[8,64,768]{2,1,0:T(8,128)(2,1)S(1)}, u32[]{:S(2)}, u32[]{:S(2)}) async-start(bf16[8,64,768]{2,1,0:T(8,128)(2,1)} %broadcast_in_dim.24), calls=%async_computation.6 | async-start | bytes 1572864 | tf_op jit(solution)/shard_map/all_to_all | solution.py:33
  7.9 12.4 %all-to-all-done.6 = bf16[8,64,768]{2,1,0:T(8,128)(2,1)S(1)} async-done(((bf16[8,64,768]{2,1,0:T(8,128)(2,1)}), bf16[8,64,768]{2,1,0:T(8,128)(2,1)S(1)}, u32[]{:S(2)}, u32[]{:S(2)}) %all-to-all-start.6) | async-done | bytes 786464 | tf_op jit(solution)/shard_map/all_to_all | solution.py:33
  20.3 0.9 broadcast_in_dim.23
  21.2 3.5 %all-to-all-start.4 = ((bf16[8,64,768]{2,1,0:T(8,128)(2,1)}), bf16[8,64,768]{2,1,0:T(8,128)(2,1)S(1)}, u32[]{:S(2)}, u32[]{:S(2)}) async-start(bf16[8,64,768]{2,1,0:T(8,128)(2,1)} %broadcast_in_dim.23), calls=%async_computation.4 | async-start | bytes 1572864 | tf_op jit(solution)/shard_map/all_to_all | solution.py:33
  24.8 5.2 %convolution_convert_fusion.2 = bf16[256,3072]{1,0:T(8,128)(2,1)} fusion(bf16[256,768]{1,0:T(8,128)(2,1)S(1)} %bitcast.51, bf16[768,3072]{1,0:T(8,128)(2,1)} %param.10), kind=kOutput, calls=%fused_computation.3 | convolution fusion | flops 1208745984 | bytes 6684672 | tf_op jit(solution)/shard_map/dot_general | solution.py:52
  30.1 6.3 %all-to-all-done.4 = bf16[8,64,768]{2,1,0:T(8,128)(2,1)S(1)} async-done(((bf16[8,64,768]{2,1,0:T(8,128)(2,1)}), bf16[8,64,768]{2,1,0:T(8,128)(2,1)S(1)}, u32[]{:S(2)}, u32[]{:S(2)}) %all-to-all-start.4) | async-done | bytes 786464 | tf_op jit(solution)/shard_map/all_to_all | solution.py:33
  36.5 5.0 %convolution_convert_fusion.3 = bf16[256,3072]{1,0:T(8,128)(2,1)} fusion(bf16[256,768]{1,0:T(8,128)(2,1)S(1)} %bitcast.45, bf16[3072,768]{1,0:T(8,128)(2,1)} %param.12), kind=kOutput, calls=%fused_computation.4 | convolution fusion | flops 1208745984 | bytes 6684672 | tf_op jit(solution)/shard_map/dot_general | solution.py:52
  41.5 0.9 broadcast_in_dim.21
  42.5 3.5 %all-to-all-start = ((bf16[8,64,768]{2,1,0:T(8,128)(2,1)}), bf16[8,64,768]{2,1,0:T(8,128)(2,1)S(1)}, u32[]{:S(2)}, u32[]{:S(2)}) async-start(bf16[8,64,768]{2,1,0:T(8,128)(2,1)} %broadcast_in_dim.21), calls=%async_computation | async-start | bytes 1572864 | tf_op jit(solution)/shard_map/all_to_all | solution.py:33
  46.0 5.4 %add_convert_fusion = bf16[256,3072]{1,0:T(8,128)(2,1)} fusion(bf16[256,3072]{1,0:T(8,128)(2,1)} %collective-permute-done.3, bf16[256,768]{1,0:T(8,128)(2,1)S(1)} %bitcast.53, bf16[768,3072]{1,0:T(8,128)(2,1)} %param.10), kind=kOutput, calls=%fused_computation.11 | convolution fusion | flops 1210318848 | bytes 8257536 | tf_op jit(solution)/shard_map/dot_general | solution.py:53
  51.4 8.8 %all-to-all-done = bf16[8,64,768]{2,1,0:T(8,128)(2,1)S(1)} async-done(((bf16[8,64,768]{2,1,0:T(8,128)(2,1)}), bf16[8,64,768]{2,1,0:T(8,128)(2,1)S(1)}, u32[]{:S(2)}, u32[]{:S(2)}) %all-to-all-start) | async-done | bytes 786464 | tf_op jit(solution)/shard_map/all_to_all | solution.py:33
  60.2 7.6 %all-to-all-start.7 = ((bf16[8,32,3072]{2,1,0:T(8,128)(2,1)}), bf16[8,32,3072]{2,1,0:T(8,128)(2,1)S(1)}, u32[]{:S(2)}, u32[]{:S(2)}) async-start(bf16[8,32,3072]{2,1,0:T(8,128)(2,1)} %bitcast.42), calls=%async_computation.7 | async-start | bytes 3145728 | tf_op jit(solution)/shard_map/all_to_all | solution.py:37
  67.8 0.8 fusion.27
  68.7 5.5 %convolution_convert_fusion.4 = bf16[256,3072]{1,0:T(8,128)(2,1)} fusion(bf16[256,768]{1,0:T(8,128)(2,1)S(1)} %bitcast.58, bf16[768,3072]{1,0:T(8,128)(2,1)} %param.10), kind=kOutput, calls=%fused_computation.5 | convolution fusion | flops 1208745984 | bytes 6684672 | tf_op jit(solution)/shard_map/dot_general | solution.py:52
  74.2 4.0 %add_convert_fusion.1 = bf16[256,3072]{1,0:T(8,128)(2,1)} fusion(bf16[256,3072]{1,0:T(8,128)(2,1)} %collective-permute-done.2, bf16[256,768]{1,0:T(8,128)(2,1)S(1)} %bitcast.48, bf16[3072,768]{1,0:T(8,128)(2,1)S(1)} %bitcast.62), kind=kOutput, calls=%fused_computation.13 | convolution fusion | flops 1210318848 | bytes 8257536 | tf_op jit(solution)/shard_map/dot_general | solution.py:53
  78.2 12.4 %all-to-all-done.7 = bf16[8,32,3072]{2,1,0:T(8,128)(2,1)S(1)} async-done(((bf16[8,32,3072]{2,1,0:T(8,128)(2,1)}), bf16[8,32,3072]{2,1,0:T(8,128)(2,1)S(1)}, u32[]{:S(2)}, u32[]{:S(2)}) %all-to-all-start.7) | async-done | bytes 1572896 | tf_op jit(solution)/shard_map/all_to_all | solution.py:37
  90.6 3.6 %all-to-all-start.5 = ((bf16[8,32,3072]{2,1,0:T(8,128)(2,1)}), bf16[8,32,3072]{2,1,0:T(8,128)(2,1)S(1)}, u32[]{:S(2)}, u32[]{:S(2)}) async-start(bf16[8,32,3072]{2,1,0:T(8,128)(2,1)} %bitcast.43), calls=%async_computation.5 | async-start | bytes 3145728 | tf_op jit(solution)/shard_map/all_to_all | solution.py:37
  94.2 5.5 %add_convert_fusion.2 = bf16[256,3072]{1,0:T(8,128)(2,1)} fusion(bf16[256,3072]{1,0:T(8,128)(2,1)} %collective-permute-done, bf16[256,768]{1,0:T(8,128)(2,1)} %bitcast.55, bf16[768,3072]{1,0:T(8,128)(2,1)} %param.10), kind=kOutput, calls=%fused_computation.15 | convolution fusion | flops 1210318848 | bytes 8257536 | tf_op jit(solution)/shard_map/dot_general | solution.py:53
  99.7 16.6 %all-to-all-done.5 = bf16[8,32,3072]{2,1,0:T(8,128)(2,1)S(1)} async-done(((bf16[8,32,3072]{2,1,0:T(8,128)(2,1)}), bf16[8,32,3072]{2,1,0:T(8,128)(2,1)S(1)}, u32[]{:S(2)}, u32[]{:S(2)}) %all-to-all-start.5) | async-done | bytes 1572896 | tf_op jit(solution)/shard_map/all_to_all | solution.py:37
  116.3 4.3 %all-to-all-start.1 = ((bf16[8,32,3072]{2,1,0:T(8,128)(2,1)}), bf16[8,32,3072]{2,1,0:T(8,128)(2,1)}, u32[]{:S(2)}, u32[]{:S(2)}) async-start(bf16[8,32,3072]{2,1,0:T(8,128)(2,1)} %bitcast.44), calls=%async_computation.1 | async-start | bytes 3145728 | tf_op jit(solution)/shard_map/all_to_all | solution.py:37
  120.6 1.0 convert_reduce_fusion.1
  121.8 20.3 %all-to-all-done.1 = bf16[8,32,3072]{2,1,0:T(8,128)(2,1)} async-done(((bf16[8,32,3072]{2,1,0:T(8,128)(2,1)}), bf16[8,32,3072]{2,1,0:T(8,128)(2,1)}, u32[]{:S(2)}, u32[]{:S(2)}) %all-to-all-start.1) | async-done | bytes 1572896 | tf_op jit(solution)/shard_map/all_to_all | solution.py:37
  142.1 1.7 convert_reduce_fusion.3
  143.8 0.4 multiply_convert_fusion
  144.4 25.0 %all_to_all.55 = bf16[8,32,3072]{2,1,0:T(8,128)(2,1)S(1)} all-to-all(bf16[8,32,3072]{2,1,0:T(8,128)(2,1)S(1)} %broadcast_in_dim.22), channel_id=1, replica_groups=mesh['x'=4,'yl'=2,'z'=4,'yh'=2,'core'=2] {'z','yh'}, dimensions={0} | all-to-all | bytes 3145728 | tf_op jit(solution)/shard_map/all_to_all | solution.py:33
  169.6 24.2 %all_to_all.56 = bf16[8,32,3072]{2,1,0:T(8,128)(2,1)S(1)} all-to-all(bf16[8,32,3072]{2,1,0:T(8,128)(2,1)S(1)} %broadcast_in_dim.25), channel_id=1, replica_groups=mesh['x'=4,'yl'=2,'z'=4,'yh'=2,'core'=2] {'z','yh'}, dimensions={0} | all-to-all | bytes 3145728 | tf_op jit(solution)/shard_map/all_to_all | solution.py:33
  193.7 1.3 broadcast_in_dim.26
  195.1 4.3 %all-to-all-start.10 = ((bf16[8,32,3072]{2,1,0:T(8,128)(2,1)}), bf16[8,32,3072]{2,1,0:T(8,128)(2,1)}, u32[]{:S(2)}, u32[]{:S(2)}) async-start(bf16[8,32,3072]{2,1,0:T(8,128)(2,1)} %broadcast_in_dim.26), calls=%async_computation.10 | async-start | bytes 3145728 | tf_op jit(solution)/shard_map/all_to_all | solution.py:33
  199.5 1.7 convert_reduce_fusion.4
  201.2 0.5 collective-permute-start.4
  201.7 18.1 %all-to-all-done.10 = bf16[8,32,3072]{2,1,0:T(8,128)(2,1)} async-done(((bf16[8,32,3072]{2,1,0:T(8,128)(2,1)}), bf16[8,32,3072]{2,1,0:T(8,128)(2,1)}, u32[]{:S(2)}, u32[]{:S(2)}) %all-to-all-start.10) | async-done | bytes 1572896 | tf_op jit(solution)/shard_map/all_to_all | solution.py:33
  219.8 3.9 %convolution_convert_fusion.8 = bf16[256,768]{1,0:T(8,128)(2,1)S(1)} fusion(bf16[256,3072]{1,0:T(8,128)(2,1)S(1)} %bitcast.41, bf16[3072,768]{1,0:T(8,128)(2,1)} %param.12), kind=kOutput, calls=%fused_computation.22 | convolution fusion | flops 1208156160 | bytes 6684672 | tf_op jit(solution)/shard_map/dot_general | solution.py:100
  223.7 2.2 convolution_convert_fusion.6
  225.9 4.2 %convolution_convert_fusion.7 = bf16[256,768]{1,0:T(8,128)(2,1)S(1)} fusion(bf16[256,3072]{1,0:T(8,128)(2,1)} %collective-permute-done.1, bf16[3072,768]{1,0:T(8,128)(2,1)} %param.12), kind=kOutput, calls=%fused_computation.21 | convolution fusion | flops 1208156160 | bytes 6684672 | tf_op jit(solution)/shard_map/dot_general | solution.py:100
  230.1 0.9 pad_maximum_fusion.2
  231.1 3.5 %all-to-all-start.3 = ((bf16[8,64,768]{2,1,0:T(8,128)(2,1)}), bf16[8,64,768]{2,1,0:T(8,128)(2,1)S(1)}, u32[]{:S(2)}, u32[]{:S(2)}) async-start(bf16[8,64,768]{2,1,0:T(8,128)(2,1)} %pad_maximum_fusion.2), calls=%async_computation.3 | async-start | bytes 1572864 | tf_op jit(solution)/shard_map/all_to_all | solution.py:37
  234.7 4.3 %convolution_convert_fusion.5 = bf16[256,768]{1,0:T(8,128)(2,1)S(1)} fusion(bf16[256,3072]{1,0:T(8,128)(2,1)} %collective-permute-done.4, bf16[768,3072]{1,0:T(8,128)(2,1)} %param.10), kind=kOutput, calls=%fused_computation.19 | convolution fusion | flops 1208156160 | bytes 6684672 | tf_op jit(solution)/shard_map/dot_general | solution.py:96
  239.0 1.0 pad_maximum_fusion.3
  240.0 6.3 %convolution_convert_fusion.1 = bf16[768,3072]{1,0:T(8,128)(2,1)} fusion(bf16[256,3072]{1,0:T(8,128)(2,1)} %collective-permute-done.4, bf16[256,3072]{1,0:T(8,128)(2,1)S(1)} %bitcast.38, bf16[256,768]{1,0:T(8,128)(2,1)S(1)} %bitcast.52, bf16[256,768]{1,0:T(8,128)(2,1)S(1)} %bitcast.54), kind=kOutput, calls=%fused_computation.2 | convolution fusion | flops 2426142720 | bytes 8650752 | tf_op jit(solution)/shard_map/dot_general | solution.py:106
  246.2 2.1 all-to-all-done.3
  248.4 3.5 %all-to-all-start.9 = ((bf16[8,64,768]{2,1,0:T(8,128)(2,1)}), bf16[8,64,768]{2,1,0:T(8,128)(2,1)S(1)}, u32[]{:S(2)}, u32[]{:S(2)}) async-start(bf16[8,64,768]{2,1,0:T(8,128)(2,1)} %pad_maximum_fusion.3), calls=%async_computation.9 | async-start | bytes 1572864 | tf_op jit(solution)/shard_map/all_to_all | solution.py:37
  251.9 2.7 convert_reduce_fusion
  254.6 6.7 %convolution_convert_fusion = bf16[3072,768]{1,0:T(8,128)(2,1)} fusion(bf16[256,3072]{1,0:T(8,128)(2,1)} %collective-permute-done.5, bf16[256,3072]{1,0:T(8,128)(2,1)} %bitcast.15, bf16[256,768]{1,0:T(8,128)(2,1)S(1)} %bitcast.47, bf16[256,768]{1,0:T(8,128)(2,1)S(1)} %bitcast.50), kind=kOutput, calls=%fused_computation.1 | convolution fusion | flops 2426142720 | bytes 8650752 | tf_op jit(solution)/shard_map/dot_general | solution.py:110
  261.5 3.0 %all-to-all-done.9 = bf16[8,64,768]{2,1,0:T(8,128)(2,1)S(1)} async-done(((bf16[8,64,768]{2,1,0:T(8,128)(2,1)}), bf16[8,64,768]{2,1,0:T(8,128)(2,1)S(1)}, u32[]{:S(2)}, u32[]{:S(2)}) %all-to-all-start.9) | async-done | bytes 786464 | tf_op jit(solution)/shard_map/all_to_all | solution.py:37
  264.6 0.7 fusion.19
  265.3 0.7 fusion.22
  (56 shorter events, 1.1 us)
Async XLA Ops:
  2.5 17.8 %all-to-all-start.6 = ((bf16[8,64,768]{2,1,0:T(8,128)(2,1)}), bf16[8,64,768]{2,1,0:T(8,128)(2,1)S(1)}, u32[]{:S(2)}, u32[]{:S(2)}) async-start(bf16[8,64,768]{2,1,0:T(8,128)(2,1)} %broadcast_in_dim.24), calls=%async_computation.6 | async-start | bytes 1572864 | tf_op jit(solution)/shard_map/all_to_all | solution.py:33
  21.2 15.2 %all-to-all-start.4 = ((bf16[8,64,768]{2,1,0:T(8,128)(2,1)}), bf16[8,64,768]{2,1,0:T(8,128)(2,1)S(1)}, u32[]{:S(2)}, u32[]{:S(2)}) async-start(bf16[8,64,768]{2,1,0:T(8,128)(2,1)} %broadcast_in_dim.23), calls=%async_computation.4 | async-start | bytes 1572864 | tf_op jit(solution)/shard_map/all_to_all | solution.py:33
  24.8 5.2 %copy-start.3 = (bf16[8,32,768]{2,1,0:T(8,128)(2,1)}, bf16[8,32,768]{2,1,0:T(8,128)(2,1)S(1)}, u32[]{:S(2)}) copy-start(bf16[8,32,768]{2,1,0:T(8,128)(2,1)S(1)} %get-tuple-element.6) | copy-start | bytes 1179652
  24.8 21.2 %copy-start.5 = (bf16[8,32,768]{2,1,0:T(8,128)(2,1)}, bf16[8,32,768]{2,1,0:T(8,128)(2,1)S(1)}, u32[]{:S(2)}) copy-start(bf16[8,32,768]{2,1,0:T(8,128)(2,1)S(1)} %get-tuple-element.7) | copy-start | bytes 1179652
  24.8 5.2 %copy-start.8 = (bf16[64,768]{1,0:T(8,128)(2,1)S(1)}, bf16[64,768]{1,0:T(8,128)(2,1)}, u32[]{:S(2)}) copy-start(bf16[64,768]{1,0:T(8,128)(2,1)} %param.7) | copy-start | bytes 294916
  30.0 16.0 %collective-permute-start.3 = (bf16[256,3072]{1,0:T(8,128)(2,1)}, bf16[256,3072]{1,0:T(8,128)(2,1)}, u32[]{:S(2)}, u32[]{:S(2)}) collective-permute-start(bf16[256,3072]{1,0:T(8,128)(2,1)} %convolution_convert_fusion.2), channel_id=1, source_target_pairs={{0,1},{1,0},{2,3},{3,2},{4,5},{5,4},{6,7},{7,6},{8,9},{9,8},{10,11... | collective-permute-start | bytes 4718600 | tf_op jit(solution)/shard_map/ppermute | solution.py:28
  36.5 37.7 %copy-start = (bf16[8,32,768]{2,1,0:T(8,128)(2,1)}, bf16[8,32,768]{2,1,0:T(8,128)(2,1)S(1)}, u32[]{:S(2)}) copy-start(bf16[8,32,768]{2,1,0:T(8,128)(2,1)S(1)} %get-tuple-element.9) | copy-start | bytes 1179652
  41.5 32.7 %collective-permute-start.2 = (bf16[256,3072]{1,0:T(8,128)(2,1)}, bf16[256,3072]{1,0:T(8,128)(2,1)}, u32[]{:S(2)}, u32[]{:S(2)}) collective-permute-start(bf16[256,3072]{1,0:T(8,128)(2,1)} %convolution_convert_fusion.3), channel_id=1, source_target_pairs={{0,1},{1,0},{2,3},{3,2},{4,5},{5,4},{6,7},{7,6},{8,9},{9,8},{10,11... | collective-permute-start | bytes 4718600 | tf_op jit(solution)/shard_map/ppermute | solution.py:28
  42.5 17.7 %all-to-all-start = ((bf16[8,64,768]{2,1,0:T(8,128)(2,1)}), bf16[8,64,768]{2,1,0:T(8,128)(2,1)S(1)}, u32[]{:S(2)}, u32[]{:S(2)}) async-start(bf16[8,64,768]{2,1,0:T(8,128)(2,1)} %broadcast_in_dim.21), calls=%async_computation | async-start | bytes 1572864 | tf_op jit(solution)/shard_map/all_to_all | solution.py:33
  60.2 30.4 %all-to-all-start.7 = ((bf16[8,32,3072]{2,1,0:T(8,128)(2,1)}), bf16[8,32,3072]{2,1,0:T(8,128)(2,1)S(1)}, u32[]{:S(2)}, u32[]{:S(2)}) async-start(bf16[8,32,3072]{2,1,0:T(8,128)(2,1)} %bitcast.42), calls=%async_computation.7 | async-start | bytes 3145728 | tf_op jit(solution)/shard_map/all_to_all | solution.py:37
  67.8 6.3 %slice-start = ((s8[4718592]{0:T(1024)(128)(4,1)}), s8[4194304]{0:T(1024)(128)(4,1)S(1)}, s32[]{:S(2)}) async-start(s8[4718592]{0:T(1024)(128)(4,1)} %bitcast.61), calls=%async_computation.11 | async-start | bytes 8388608
  68.7 5.5 %slice-start.1 = ((s8[4718592]{0:T(1024)(128)(4,1)}), s8[524288]{0:T(1024)(128)(4,1)S(1)}, s32[]{:S(2)}) async-start(s8[4718592]{0:T(1024)(128)(4,1)} %bitcast.61), calls=%async_computation.12 | async-start | bytes 1048576
  74.2 20.0 %collective-permute-start = (bf16[256,3072]{1,0:T(8,128)(2,1)}, bf16[256,3072]{1,0:T(8,128)(2,1)}, u32[]{:S(2)}, u32[]{:S(2)}) collective-permute-start(bf16[256,3072]{1,0:T(8,128)(2,1)} %convolution_convert_fusion.4), channel_id=1, source_target_pairs={{0,1},{1,0},{2,3},{3,2},{4,5},{5,4},{6,7},{7,6},{8,9},{9,8},{10,11... | collective-permute-start | bytes 4718600 | tf_op jit(solution)/shard_map/ppermute | solution.py:28
  90.6 25.7 %all-to-all-start.5 = ((bf16[8,32,3072]{2,1,0:T(8,128)(2,1)}), bf16[8,32,3072]{2,1,0:T(8,128)(2,1)S(1)}, u32[]{:S(2)}, u32[]{:S(2)}) async-start(bf16[8,32,3072]{2,1,0:T(8,128)(2,1)} %bitcast.43), calls=%async_computation.5 | async-start | bytes 3145728 | tf_op jit(solution)/shard_map/all_to_all | solution.py:37
  116.3 25.8 %all-to-all-start.1 = ((bf16[8,32,3072]{2,1,0:T(8,128)(2,1)}), bf16[8,32,3072]{2,1,0:T(8,128)(2,1)}, u32[]{:S(2)}, u32[]{:S(2)}) async-start(bf16[8,32,3072]{2,1,0:T(8,128)(2,1)} %bitcast.44), calls=%async_computation.1 | async-start | bytes 3145728 | tf_op jit(solution)/shard_map/all_to_all | solution.py:37
  120.6 23.2 %copy-start.9 = (f32[3072]{0:T(1024)S(1)}, f32[3072]{0:T(1024)}, u32[]{:S(2)}) copy-start(f32[3072]{0:T(1024)} %param.11) | copy-start | bytes 36868
  121.6 22.2 %copy-start.2 = (f32[32,3072]{1,0:T(8,128)S(1)}, f32[32,3072]{1,0:T(8,128)}, u32[]{:S(2)}) copy-start(f32[32,3072]{1,0:T(8,128)} %convert_reduce_fusion.1) | copy-start | bytes 1179652
  195.1 24.8 %all-to-all-start.10 = ((bf16[8,32,3072]{2,1,0:T(8,128)(2,1)}), bf16[8,32,3072]{2,1,0:T(8,128)(2,1)}, u32[]{:S(2)}, u32[]{:S(2)}) async-start(bf16[8,32,3072]{2,1,0:T(8,128)(2,1)} %broadcast_in_dim.26), calls=%async_computation.10 | async-start | bytes 3145728 | tf_op jit(solution)/shard_map/all_to_all | solution.py:33
  199.4 26.5 %collective-permute-start.1 = (bf16[256,3072]{1,0:T(8,128)(2,1)S(1)}, bf16[256,3072]{1,0:T(8,128)(2,1)}, u32[]{:S(2)}, u32[]{:S(2)}) collective-permute-start(bf16[256,3072]{1,0:T(8,128)(2,1)S(1)} %bitcast.40), channel_id=1, source_target_pairs={{0,1},{1,0},{2,3},{3,2},{4,5},{5,4},{6,7},{7,6},{8,9},{9,8},{10,11... | collective-permute-start | bytes 4718600 | tf_op jit(solution)/shard_map/ppermute | solution.py:28
  201.2 33.4 %collective-permute-start.4 = (bf16[256,3072]{1,0:T(8,128)(2,1)S(1)}, bf16[256,3072]{1,0:T(8,128)(2,1)}, u32[]{:S(2)}, u32[]{:S(2)}) collective-permute-start(bf16[256,3072]{1,0:T(8,128)(2,1)S(1)} %bitcast.36), channel_id=1, source_target_pairs={{0,1},{1,0},{2,3},{3,2},{4,5},{5,4},{6,7},{7,6},{8,9},{9,8},{10,11... | collective-permute-start | bytes 4718600 | tf_op jit(solution)/shard_map/ppermute | solution.py:28
  219.8 3.9 %slice-start.2 = ((s8[4718592]{0:T(1024)(128)(4,1)}), s8[4194304]{0:T(1024)(128)(4,1)S(1)}, s32[]{:S(2)}) async-start(s8[4718592]{0:T(1024)(128)(4,1)} %bitcast.63), calls=%async_computation.13 | async-start | bytes 8388608
  219.8 3.9 %slice-start.3 = ((s8[4718592]{0:T(1024)(128)(4,1)}), s8[524288]{0:T(1024)(128)(4,1)S(1)}, s32[]{:S(2)}) async-start(s8[4718592]{0:T(1024)(128)(4,1)} %bitcast.63), calls=%async_computation.14 | async-start | bytes 1048576
  219.8 34.8 %collective-permute-start.5 = (bf16[256,3072]{1,0:T(8,128)(2,1)}, bf16[256,3072]{1,0:T(8,128)(2,1)}, u32[]{:S(2)}, u32[]{:S(2)}) collective-permute-start(bf16[256,3072]{1,0:T(8,128)(2,1)} %bitcast.15), channel_id=1, source_target_pairs={{0,1},{1,0},{2,3},{3,2},{4,5},{5,4},{6,7},{7,6},{8,9},{9,8},{10,11... | collective-permute-start | bytes 4718600 | tf_op jit(solution)/shard_map/ppermute | solution.py:28
  231.1 17.3 %all-to-all-start.3 = ((bf16[8,64,768]{2,1,0:T(8,128)(2,1)}), bf16[8,64,768]{2,1,0:T(8,128)(2,1)S(1)}, u32[]{:S(2)}, u32[]{:S(2)}) async-start(bf16[8,64,768]{2,1,0:T(8,128)(2,1)} %pad_maximum_fusion.2), calls=%async_computation.3 | async-start | bytes 1572864 | tf_op jit(solution)/shard_map/all_to_all | solution.py:37
  234.6 4.4 %copy-start.7 = (bf16[256,768]{1,0:T(8,128)(2,1)S(1)}, bf16[256,768]{1,0:T(8,128)(2,1)}, u32[]{:S(2)}) copy-start(bf16[256,768]{1,0:T(8,128)(2,1)} %convolution_convert_fusion.6) | copy-start | bytes 1179652
  234.6 5.3 %copy-start.4 = (bf16[8,32,768]{2,1,0:T(8,128)(2,1)S(1)}, bf16[8,32,768]{2,1,0:T(8,128)(2,1)}, u32[]{:S(2)}) copy-start(bf16[8,32,768]{2,1,0:T(8,128)(2,1)} %copy-done.3) | copy-start | bytes 1179652
  234.6 5.3 %copy-start.6 = (bf16[8,32,768]{2,1,0:T(8,128)(2,1)S(1)}, bf16[8,32,768]{2,1,0:T(8,128)(2,1)}, u32[]{:S(2)}) copy-start(bf16[8,32,768]{2,1,0:T(8,128)(2,1)} %copy-done.5) | copy-start | bytes 1179652
  248.4 16.1 %all-to-all-start.9 = ((bf16[8,64,768]{2,1,0:T(8,128)(2,1)}), bf16[8,64,768]{2,1,0:T(8,128)(2,1)S(1)}, u32[]{:S(2)}, u32[]{:S(2)}) async-start(bf16[8,64,768]{2,1,0:T(8,128)(2,1)} %pad_maximum_fusion.3), calls=%async_computation.9 | async-start | bytes 1572864 | tf_op jit(solution)/shard_map/all_to_all | solution.py:37
  251.9 2.7 %copy-start.1 = (bf16[8,32,768]{2,1,0:T(8,128)(2,1)S(1)}, bf16[8,32,768]{2,1,0:T(8,128)(2,1)}, u32[]{:S(2)}) copy-start(bf16[8,32,768]{2,1,0:T(8,128)(2,1)} %copy-done) | copy-start | bytes 1179652
  254.6 10.7 %copy-start.10 = (f32[768]{0:T(1024)S(1)}, f32[768]{0:T(1024)}, u32[]{:S(2)}) copy-start(f32[768]{0:T(1024)} %param.13) | copy-start | bytes 9220

commit v2 on v1

v2 whole, which is shorter than its diff:
```python
import functools

import jax
import jax.numpy as jnp
from jax import lax
from jax.experimental import pallas as pl
from jax.experimental.pallas import tpu as pltpu
from jax.sharding import Mesh, PartitionSpec as P

coeff = 0.7978845608
plain = (((1,), (0,)), ((), ()))
outer = (((0,), (0,)), ((), ()))
inner = (((1,), (1,)), ((), ()))
ROW = ("x", "yl")
CHIPS = ("z", "yh")
COL = ("z", "yh", "core")
f32 = jnp.float32
bf16 = jnp.bfloat16
VMEM_LIMIT = 40 << 20
ALL_VMEM = 61 << 20
MICRO = 3_000
TILE = 512


def gelu_tanh(values):
    return 0.5 * values * (1.0 + jnp.tanh(coeff * (values + 0.044715 * values * values * values)))


def gelu_slope(values):
    tangent = jnp.tanh(coeff * (values + 0.044715 * values * values * values))
    return 0.5 * (1.0 + tangent) + 0.5 * values * (1.0 - tangent * tangent) * coeff * (
        1.0 + 3.0 * 0.044715 * values * values
    )


def swap(values, axis="core", name="core_swap"):
    with jax.named_scope(name):
        return lax.ppermute(values, axis, [(0, 1), (1, 0)])


def whole(array):
    return pl.BlockSpec(array.shape, lambda j, core: (0,) * len(array.shape))


def tiled(array, axis, tile, at=lambda j, core: j):
    shape = array.shape[:axis] + (tile,) + array.shape[axis + 1 :]
    return pl.BlockSpec(shape, lambda j, core: tuple(at(j, core[0]) if i == axis else 0 for i in range(len(shape))))


def last(array, tile, at=lambda j, core: j):
    return tiled(array, len(array.shape) - 1, tile, at)


def like(shape, dtype=bf16):
    return jax.ShapeDtypeStruct(shape, dtype)


def call(body, steps, operands, in_specs, shapes, out_specs, waits=(), scratch=(), micros=1, limit=VMEM_LIMIT):
    used = len(operands)
    name = body.__qualname__.split(".")[0]

    def kernel(core, *refs):
        body(*refs[:used], *refs[used + len(waits) :])

    return pl.pallas_call(
        kernel,
        name=name,
        grid_spec=pltpu.PrefetchScalarGridSpec(
            num_scalar_prefetch=1,
            grid=(steps,),
            in_specs=[*in_specs, *[pl.BlockSpec(memory_space=pl.ANY)] * len(waits)],
            out_specs=out_specs,
            scratch_shapes=scratch,
        ),
        out_shape=shapes,
        compiler_params=pltpu.CompilerParams(vmem_limit_bytes=limit),
        cost_estimate=pl.CostEstimate(flops=0, bytes_accessed=micros * MICRO, transcendentals=0),
    )(lax.axis_index("core").astype(jnp.int32)[None], *operands, *waits)


def spread_kernel(x, out):
    sub = out.shape[2]
    for a in range(2):
        piece = x[pl.ds(pl.multiple_of((lax.axis_index("yh") ^ a) * sub, sub), sub), :]
        for i in range(out.shape[0]):
            out[i, a] = piece


def tokens_of(values, name, waits=()):
    count, width = values.shape
    shape = like((lax.axis_size(ROW), 2, count // 2, width))
    (copies,) = call(spread_kernel, 1, [values], [whole(values)], [shape], [whole(shape)], waits)
    with jax.named_scope(name):
        return lax.all_to_all(copies, ROW, 0, 0), copies


def tokens_of_chip(values, waits=()):
    def body(x, out):
        sub = out.shape[1]
        for a in range(2):
            out[a] = x[pl.ds(pl.multiple_of((lax.axis_index("yh") ^ a) * sub, sub), sub), :]

    count, width = values.shape
    ordered = simple(body, [values], [like((2, count // 2, width))], waits)[0]
    found = lax.all_gather(ordered, (*ROW, "core"), axis=0, tiled=False)
    return found.reshape(-1, 2, *ordered.shape)


def settle_kernel(parts, bias, out):
    sub = parts.shape[1] // 2
    total = jnp.sum(parts[...].astype(f32), axis=0) + bias[...]
    for a in range(2):
        at = pl.ds(pl.multiple_of((lax.axis_index("yh") ^ a) * sub, sub), sub)
        out[at, :] = total[a * sub : (a + 1) * sub].astype(bf16)


def sum_hidden(parts, bias, name, waits=()):
    rows, subs, sub, width = parts.shape
    with jax.named_scope(name):
        got = lax.all_to_all(parts, ROW, 0, 0).reshape(rows, subs * sub, width)
    shape = like((subs * sub, width))
    (out,) = call(settle_kernel, 1, [got, bias], [whole(got), whole(bias)], [shape], [whole(shape)], waits)
    return out


def rows_of(ref):
    rows, _, sub, width = ref.shape
    return jnp.concatenate([ref[:, a].reshape(rows * sub, width) for a in range(2)], 0)


IN_HBM = pl.BlockSpec(memory_space=pltpu.HBM)


def part_of(weight, axis, start, size):
    at = pl.ds(pl.multiple_of(start, size), size)
    return weight.at[:, at] if axis else weight.at[at, :]


def exchanged(weight, axis, waits, tile=TILE):
    def body(part, out):
        out[...] = part[...]

    half = weight.shape[axis] // 2
    steps = half // tile
    shape = like(weight.shape[:axis] + (half,) + weight.shape[axis + 1 :])
    spec = tiled(weight, axis, tile, lambda j, core: (1 - core) * steps + j)
    return swap(call(body, steps, [weight], [spec], [shape], [tiled(shape, axis, tile)], waits)[0])


def fetched(pairs, axis, tile, steps):
    shapes = [a.shape[:axis] + (tile,) + a.shape[axis + 1 :] for a in pairs]
    scratch = [pltpu.VMEM((steps,) + shape, bf16) for shape in shapes]
    scratch += [pltpu.SemaphoreType.DMA((steps,)) for _ in pairs]

    def get(refs, firsts, buffers, sems):
        step = pl.program_id(0)

        def copy(k, j):
            return pltpu.make_async_copy(
                part_of(refs[k], axis, (firsts[k] + j) * tile, tile), buffers[k].at[j], sems[k].at[j]
            )

        @pl.when(step == 0)
        def _():
            for j in range(steps):
                for k in range(len(refs)):
                    copy(k, j).start()

        for k in range(len(refs)):
            copy(k, step).wait()
        return [buffer[step] for buffer in buffers]

    return scratch, get


def up(x, w, w_far, dims, kind, waits=(), tile=TILE):
    axis = 1 if dims == plain else 0
    half = w_far.shape[axis]
    steps = half // tile
    chips = lax.axis_size("z")

    scratch, get = fetched([w, w_far], axis, tile, steps)

    def body(x, x_far, *refs):
        *outs, own, own_far, sem, sem_far = refs[2:]
        w, w_far = get(refs[:2], [lax.axis_index("core") * steps, 0], [own, own_far], [sem, sem_far])
        term = lax.dot_general(rows_of(x), w, dims, preferred_element_type=f32)
        term += lax.dot_general(rows_of(x_far), w_far, dims, preferred_element_type=f32)
        count = term.shape[0] // 2
        for a in range(2):
            part = term[a * count : (a + 1) * count].astype(bf16)
            if kind == "pair":
                outs[a][...] = part
            else:
                outs[0][:, a] = part.reshape(chips, count // chips, tile)

    if len(x) == 2:
        specs = [whole(x[0]), whole(x[1])]
    else:
        x = (x[0], x[0])
        rows, _, subs, sub, width = x[0].shape
        specs = [pl.BlockSpec((rows, None, subs, sub, width), lambda j, core, k=k: (0, core[0] ^ k, 0, 0, 0)) for k in range(2)]
    rows, subs, sub, width = x[0].shape[-4:] if len(x[0].shape) == 4 else (x[0].shape[0], *x[0].shape[2:])
    if kind == "pair":
        shapes = [like((rows * sub, half))] * 2
    else:
        shapes = [like((chips, 2, rows * sub // chips, half))]
    specs += [IN_HBM, IN_HBM]
    return call(body, steps, [*x, w, w_far], specs, shapes, [last(s, tile) for s in shapes], waits, scratch, 5, ALL_VMEM)


def all_rows(refs, kind):
    if kind == "quarters":
        return jnp.concatenate([ref[...] for ref in refs], 0)
    (ref,) = refs
    chips, _, block, width = ref.shape
    order = [a if kind == "relative" else lax.axis_index("yh") ^ a for a in range(2)]
    return jnp.concatenate([ref[:, pl.ds(at, 1)].reshape(chips * block, width) for at in order], 0)


def down(full, w, dims, x, waits=(), tile=TILE):
    near, far, kind = full
    axis = 0 if dims == plain else 1
    steps = near[0].shape[-1] // tile
    count = len(near)

    scratch, get = fetched([w, w], axis, tile, steps)

    def body(*refs):
        *parts, w, out, total, own, own_far, sem, sem_far = refs
        step = pl.program_id(0)
        core = lax.axis_index("core")
        w_near, w_far = get([w, w], [core * steps, (1 - core) * steps], [own, own_far], [sem, sem_far])
        term = lax.dot_general(all_rows(parts[:count], kind), w_near, dims, preferred_element_type=f32)
        term += lax.dot_general(all_rows(parts[count:], kind), w_far, dims, preferred_element_type=f32)

        @pl.when(step == 0)
        def _():
            total[...] = term

        @pl.when(step > 0)
        def _():
            total[...] += term

        @pl.when(step == steps - 1)
        def _():
            rows, _, sub, width = out.shape
            for a in range(2):
                out[:, a] = total[a * rows * sub : (a + 1) * rows * sub].astype(bf16).reshape(rows, sub, width)

    shape = like(x.shape)
    specs = [last(h, tile) for h in (*near, *far)]
    specs += [IN_HBM]
    scratch = [pltpu.VMEM((x.size // x.shape[-1], x.shape[-1]), f32), *scratch]
    return call(body, steps, [*near, *far, w], specs, [shape], [whole(shape)], waits, scratch, 6, ALL_VMEM)[0]


def grad(x, full, along, sums=False, waits=(), tile=TILE):
    near, far, kind = full
    half, width = near[0].shape[-1], x.shape[-1]
    steps = half // tile
    count = len(near)

    def body(x, *refs):
        parts, outs = refs[: 2 * count], refs[2 * count :]

        def one(refs):
            values = all_rows(refs, kind)
            pair = (values, rows_of(x)) if along == 0 else (rows_of(x), values)
            outs[0][...] = lax.dot_general(*pair, outer, preferred_element_type=f32).astype(bf16)
            if sums:
                outs[1][...] = jnp.sum(values.astype(f32), axis=0, keepdims=True)

        @pl.when(pl.program_id(0) < steps)
        def _():
            one(parts[:count])

        @pl.when(pl.program_id(0) >= steps)
        def _():
            one(parts[count:])

    def place(j, core):
        return jnp.where(j < steps, core * steps + j, (1 - core) * steps + j - steps)

    shape = like((width, 2 * half) if along else (2 * half, width))
    shapes = [shape] + ([like((1, 2 * half), f32)] if sums else [])
    out_specs = [tiled(shape, along, tile, place)] + ([last(shapes[1], tile, place)] if sums else [])
    specs = [whole(x), *[last(h, tile, lambda j, core: jnp.minimum(j, steps - 1)) for h in near]]
    specs += [last(h, tile, lambda j, core: jnp.maximum(j - steps, 0)) for h in far]
    return call(body, 2 * steps, [x, *near, *far], specs, shapes, out_specs, waits, (), 6)


def simple(body, operands, shapes, waits=()):
    return call(body, 1, operands, [whole(o) for o in operands], shapes, [whole(s) for s in shapes], waits)


def add_far(kept, got, waits=()):
    def body(kept, got, out):
        out[...] = (kept[...].astype(f32) + got[...].astype(f32)).astype(bf16)

    return simple(body, [kept, got], [like(kept.shape)], waits)[0]


def halves_of(got, waits=()):
    def body(got, kept, sent):
        kept[...] = jnp.sum(got[:, 0].astype(f32), axis=0)
        sent[...] = jnp.sum(got[:, 1].astype(f32), axis=0).astype(bf16)

    return simple(body, [got], [like(got.shape[2:], f32), like(got.shape[2:])], waits)


def finish_b(near, far, bias, waits=()):
    def body(near, far, bias, pre, out):
        values = near[...] + far[...].astype(f32) + bias[...]
        pre[...] = values
        out[...] = gelu_tanh(values).astype(bf16)

    return simple(body, [near, far, bias], [like(near.shape, f32), like(near.shape)], waits)


def finish_a(got, bias, copies, waits=()):
    def body(got, bias, out):
        values = gelu_tanh(jnp.sum(got[...].astype(f32), axis=0) + bias[...]).astype(bf16)
        for i in range(copies):
            out[i] = values

    return simple(body, [got, bias], [like((copies,) + got.shape[1:])], waits)[0]


def finish_back(got, pre, copies, waits=()):
    def body(got, pre, out):
        back = jnp.sum(got[...].astype(f32), axis=0)
        values = (back * gelu_slope(pre[...])).astype(bf16)
        for i in range(copies):
            out[i] = values

    return simple(body, [got, pre], [like((copies,) + pre.shape)], waits)[0]


def paired(near, far, copies, waits=()):
    def body(near, far, out):
        for i in range(copies):
            out[i, 0] = near[...]
            out[i, 1] = far[...]

    return simple(body, [near, far], [like((copies, 2) + near.shape)], waits)[0]


def relay(values, waits):
    def body(x, out):
        out[...] = x[...]

    return simple(body, [values], [like(values.shape)], waits)[0]


def along_z(values, name):
    with jax.named_scope(name):
        return lax.all_to_all(values, "z", 0, 0)


def gather_near(copies, name, waits=()):
    near = along_z(copies, name + "_z").reshape(-1, copies.shape[-1])
    far = swap(near, "yh", name + "_y")
    passed = relay(far, waits) if waits else far
    return [near, far], [swap(near), swap(passed)], "quarters"


def gather_far(values, name, waits=(), waits_core=()):
    mine = along_z(paired(values, swap(values, "yh", name + "_y"), lax.axis_size("z"), waits), name + "_z")
    passed = relay(mine, waits_core) if waits_core else mine
    return [mine], [swap(passed)], "relative"


def per_device(input_a, input_b, cotangent, weight_in, bias_in, weight_out, bias_out):
    hidden = weight_in.shape[1]
    chips = lax.axis_size("z")
    bias_out = bias_out[None]
    bias_half = lax.dynamic_slice_in_dim(bias_in, lax.axis_index("core") * (hidden // 2), hidden // 2)[None]

    x_a, _ = tokens_of(input_a, "row_a")
    x_b, _ = tokens_of(input_b, "row_b")
    x_cot, _ = tokens_of(cotangent, "row_cot")
    far_in = exchanged(weight_in, 1, [x_a])

    kept_a, sent_a = up([x_a, swap(x_a)], weight_in, far_in, plain, "pair")
    far_out = exchanged(weight_out, 0, [kept_a])
    (term_b,) = up([x_b, swap(relay(x_b, [kept_a]))], weight_in, far_in, plain, "relative")
    kept_cot, sent_cot = up([x_cot, swap(relay(x_cot, [term_b]))], weight_out, far_out, inner, "pair")

    near_b, sent_b = halves_of(along_z(term_b, "sum_b_z"), [kept_cot])
    both_a = add_far(kept_a, swap(sent_a, "yh", "sum_a_y"), [near_b])
    got_a = along_z(both_a.reshape(chips, -1, hidden // 2), "sum_a_z")
    both_cot = add_far(kept_cot, swap(sent_cot, "yh", "sum_cot_y"))
    pre_b, hidden_b = finish_b(near_b, swap(sent_b, "yh", "sum_b_y"), bias_half)
    copies_a = finish_a(got_a, bias_half, chips, [pre_b])
    full_a = gather_near(copies_a, "all_a")
    got_cot = along_z(both_cot.reshape(chips, -1, hidden // 2), "sum_cot_z")
    copies_back = finish_back(got_cot, pre_b, chips, [copies_a])

    parts_a = down(full_a, weight_out, plain, x_b, [copies_back])
    full_back = gather_near(copies_back, "all_back", [parts_a])
    full_b = gather_far(hidden_b, "all_b", [full_a[0][1], full_back[0][0]], [parts_a, full_back[0][1]])
    (grad_weight_out,) = grad(x_cot, full_b, 0, False, [parts_a])
    parts_back = down(full_back, weight_in, inner, x_b, [grad_weight_out])
    grad_weight_in, sums = grad(x_b, full_back, 1, True, [parts_back])
    output_a = sum_hidden(parts_a, bias_out, "row_out")
    grad_input = sum_hidden(parts_back, jnp.zeros_like(bias_out), "row_in")
    grad_bias_out = jnp.sum(x_cot.reshape(-1, x_cot.shape[-1]).astype(f32), axis=0)
    return (output_a, grad_input, grad_weight_in, sums[0], grad_weight_out, grad_bias_out)


def solution(mesh):
    fine = Mesh(mesh.devices.reshape(4, 2, 4, 2, 2), ("x", "yl", "z", "yh", "core"))
    return jax.shard_map(
        per_device,
        mesh=fine,
        in_specs=(
            P(ROW, COL),
            P(ROW, COL),
            P(ROW, COL),
            P(COL, ROW),
            P(ROW),
            P(ROW, COL),
            P(COL),
        ),
        out_specs=(
            P(ROW, COL),
            P(ROW, COL),
            P(COL, ROW),
            P(ROW),
            P(ROW, COL),
            P(COL),
        ),
        check_vma=False,
    )
```

time: 267 us -> 224 us (0.84)
  Pallas kernels: 0 us -> 67.3 us
  matrix products: 58.2 us -> 0 us
  waiting for transfers between devices: 100 us -> 60.4 us
  blocking collectives: 49.1 us -> 17.7 us
  starting transfers between devices: 40 us -> 61.3 us
  other arithmetic: 11.2 us -> 0.74 us
  local copies, waits for them, and re-layouts: 6.37 us -> 13.7 us
    all_to_all x9 -> x10, waiting for transfers between devices: 100 us -> 31.3 us  [the longest x6 23.6 us: along_z(): return lax.all_to_all(values, 'z', 0, 0)]
    pallas_call x0 -> x25, Pallas kernels: none -> 67.3 us  [call(): pl.pallas_call(kernel, name=name, grid_spec=pltpu.PrefetchScalarGridSpec(...]
    dot_general x12 -> x0, matrix products: 58.2 us -> none  [the longest x3 15.7 us: sum_features(): lax.dot_general(other, weight, dims, preferred_element_type=f32)]
    all_to_all x2 -> x1, blocking collectives: 49.1 us -> 17.7 us  [tokens_of(): return (lax.all_to_all(copies, ROW, 0, 0), copies)]
    ppermute x6 -> x16, waiting for transfers between devices: 0.02 us -> 29.2 us  [swap(): return lax.ppermute(values, axis, [(0, 1), (1, 0)])]
    ppermute x6 -> x16, starting transfers between devices: 0.59 us -> 17.7 us  [swap(): return lax.ppermute(values, axis, [(0, 1), (1, 0)])]
    unnamed x30 -> x50, local copies, waits for them, and re-layouts: 0.07 us -> 13.6 us
    reduce_sum x7 -> x1, other arithmetic: 7.45 us -> 0.74 us  [per_device(): jnp.sum(x_cot.reshape(-1, x_cot.shape[-1]).astype(f32), axis=0)]
  transfers between devices with their start and end apart: 15 -> 26, of which waited for: 9 -> 14; matrix products, arithmetic and copies ran while one was open for 25% -> 0% of each run, Pallas kernels for 0% -> 27%
where the time goes in v2:
time: 224 us; the launch traced here: 222 us
  Pallas kernels  67.3 us (30%)
  starting transfers between devices  61.3 us (27%)
  waiting for transfers between devices  60.4 us (27%)
  blocking collectives  17.7 us (8%)
  local copies, waits for them, and re-layouts  13.7 us (6%)
    pallas_call x25, Pallas kernels, call(): pl.pallas_call(kernel, name=name, grid_spec=pltpu.PrefetchScalarGridSpec(...  67.3 us
    ppermute x16, waiting for transfers between devices, swap(): return lax.ppermute(values, axis, [(0, 1), (1, 0)])  29.2 us
    all_to_all x6, starting transfers between devices, along_z(): return lax.all_to_all(values, 'z', 0, 0)  24.8 us
    all_to_all x6, waiting for transfers between devices, along_z(): return lax.all_to_all(values, 'z', 0, 0)  23.6 us
    all_to_all x1, blocking collectives, tokens_of(): return (lax.all_to_all(copies, ROW, 0, 0), copies)  17.7 us
    ppermute x16, starting transfers between devices, swap(): return lax.ppermute(values, axis, [(0, 1), (1, 0)])  17.7 us
    unnamed x50, local copies, waits for them, and re-layouts  13.6 us
    all_to_all x2, starting transfers between devices, sum_hidden(): got = lax.all_to_all(parts, ROW, 0, 0).reshape(rows, subs * sub, width)  9.95 us
  transfers between devices with their start and end apart: 26, of which 14 were waited for; matrix products, arithmetic and copies ran while one was open for 0% of the time, Pallas kernels for 27%

profile of v2, /device:TPU:0, one launch (start us, length us, event | category | flops | bytes accessed | tf_op | source)
XLA Modules:
  0.0 222.1 jit_solution(11043280972752365338)
XLA Ops:
  1.6 17.7 %all_to_all.55.refs_1_.refs_0_ = bf16[8,2,32,768]{3,2,1,0:T(8,128)(2,1)S(1)} all-to-all(bf16[8,2,32,768]{3,2,1,0:T(8,128)(2,1)S(1)} %spread_kernel.3), channel_id=1, replica_groups=mesh['x'=4,'yl'=2,'z'=4,'yh'=2,'core'=2] {'x','yl'}, dimensions={0} | all-to-all | bytes 1572864 | tf_op jit(solution)/shard_map/row_a/all_to_all | solution.py:94
  19.3 2.3 %copy-done = bf16[768,3072]{1,0:T(8,128)(2,1)S(1)} copy-done((bf16[768,3072]{1,0:T(8,128)(2,1)S(1)}, bf16[768,3072]{1,0:T(8,128)(2,1)}, u32[]{:S(2)}) %copy-start) | copy-done | bytes 4718616
  21.7 2.1 exchanged.2
  25.2 3.5 %all-to-all-start.1 = ((bf16[8,2,32,768]{3,2,1,0:T(8,128)(2,1)}), bf16[8,2,32,768]{3,2,1,0:T(8,128)(2,1)S(1)}, u32[]{:S(2)}, u32[]{:S(2)}) async-start(bf16[8,2,32,768]{3,2,1,0:T(8,128)(2,1)} %spread_kernel.4), calls=%async_computation.1 | async-start | bytes 1572864 | tf_op jit(solution)/shard_map/row_b/all_to_all | solution.py:94
  29.9 6.8 %up.3 = (bf16[256,1536]{1,0:T(8,128)(2,1)}, bf16[256,1536]{1,0:T(8,128)(2,1)}) custom-call(s32[1]{0:T(128)} %bitcast.core, bf16[8,2,32,768]{3,2,1,0:T(8,128)(2,1)} %copy-done.13, bf16[8,2,32,768]{3,2,1,0:T(8,128)(2,1)} %copy-done.21, bf16[768,3072]{1,0:T(8,128)(2,1)} %refs_4_.3, bf16[768,1536]{1,0:T(8,128)(2,1)} %collective-permute-done.1.refs_3_), custom_call_target="tpu_custom_call" | custom-call | bytes 15000 | tf_op jit(solution)/shard_map/up/pallas_call | solution.py:65
  36.8 2.3 %copy-done.1 = bf16[3072,768]{1,0:T(8,128)(2,1)S(1)} copy-done((bf16[3072,768]{1,0:T(8,128)(2,1)S(1)}, bf16[3072,768]{1,0:T(8,128)(2,1)}, u32[]{:S(2)}) %copy-start.1) | copy-done | bytes 4718616
  39.1 1.1 copy-done.10
  40.2 1.9 exchanged.3
  44.0 5.4 %all-to-all-start.3 = ((bf16[8,2,32,768]{3,2,1,0:T(8,128)(2,1)}), bf16[8,2,32,768]{3,2,1,0:T(8,128)(2,1)S(1)}, u32[]{:S(2)}, u32[]{:S(2)}) async-start(bf16[8,2,32,768]{3,2,1,0:T(8,128)(2,1)} %spread_kernel.5), calls=%async_computation.3 | async-start | bytes 1572864 | tf_op jit(solution)/shard_map/row_cot/all_to_all | solution.py:94
  49.4 6.9 %up.4.refs_1_ = bf16[4,2,64,1536]{3,2,1,0:T(8,128)(2,1)} custom-call(s32[1]{0:T(128)} %bitcast.core, bf16[8,2,32,768]{3,2,1,0:T(8,128)(2,1)} %copy-done.5, bf16[8,2,32,768]{3,2,1,0:T(8,128)(2,1)} %collective-permute-done.3.refs_1_, bf16[768,3072]{1,0:T(8,128)(2,1)} %refs_4_.3, bf16[768,1536]{1,0:T(8,128)(2,1)} %collective-permute-done.1.refs_3_), custom_call_target="tpu_custom_call" | custom-call | bytes 15000 | tf_op jit(solution)/shard_map/up/pallas_call | solution.py:65
  56.3 5.5 %all-to-all-done.3.refs_0_ = bf16[8,2,32,768]{3,2,1,0:T(8,128)(2,1)S(1)} async-done(((bf16[8,2,32,768]{3,2,1,0:T(8,128)(2,1)}), bf16[8,2,32,768]{3,2,1,0:T(8,128)(2,1)S(1)}, u32[]{:S(2)}, u32[]{:S(2)}) %all-to-all-start.3) | async-done | bytes 786464 | tf_op jit(solution)/shard_map/row_cot/all_to_all | solution.py:94
  61.7 5.3 %all-to-all-start.2 = ((bf16[4,2,64,1536]{3,2,1,0:T(8,128)(2,1)}), bf16[4,2,64,1536]{3,2,1,0:T(8,128)(2,1)}, u32[]{:S(2)}, u32[]{:S(2)}) async-start(bf16[4,2,64,1536]{3,2,1,0:T(8,128)(2,1)} %up.4.refs_1_), calls=%async_computation.2 | async-start | bytes 3145728 | tf_op jit(solution)/shard_map/sum_b_z/all_to_all | solution.py:358
  67.2 3.0 %collective-permute-start.2 = (bf16[256,1536]{1,0:T(8,128)(2,1)}, bf16[256,1536]{1,0:T(8,128)(2,1)S(1)}, u32[]{:S(2)}, u32[]{:S(2)}) collective-permute-start(bf16[256,1536]{1,0:T(8,128)(2,1)} %get-tuple-element.17), channel_id=1, source_target_pairs={{0,2},{2,0},{1,3},{3,1},{4,6},{6,4},{5,7},{7,5},{8,10},{10,8},{9,1... | collective-permute-start | bytes 2359304 | tf_op jit(solution)/shard_map/sum_a_y/ppermute | solution.py:38
  71.2 7.1 %up.5 = (bf16[256,1536]{1,0:T(8,128)(2,1)}, bf16[256,1536]{1,0:T(8,128)(2,1)}) custom-call(s32[1]{0:T(128)} %bitcast.core, bf16[8,2,32,768]{3,2,1,0:T(8,128)(2,1)} %copy-done.2, bf16[8,2,32,768]{3,2,1,0:T(8,128)(2,1)} %copy-done.22, bf16[3072,768]{1,0:T(8,128)(2,1)} %refs_4_.2, bf16[1536,768]{1,0:T(8,128)(2,1)} %collective-permute-done.5.refs_3_), custom_call_target="tpu_custom_call" | custom-call | bytes 15000 | tf_op jit(solution)/shard_map/up/pallas_call | solution.py:65
  78.3 8.5 %all-to-all-done.2.refs_0_ = bf16[4,2,64,1536]{3,2,1,0:T(8,128)(2,1)} async-done(((bf16[4,2,64,1536]{3,2,1,0:T(8,128)(2,1)}), bf16[4,2,64,1536]{3,2,1,0:T(8,128)(2,1)}, u32[]{:S(2)}, u32[]{:S(2)}) %all-to-all-start.2) | async-done | bytes 1572896 | tf_op jit(solution)/shard_map/sum_b_z/all_to_all | solution.py:358
  86.9 1.1 copy-done.16
  88.0 1.6 halves_of.1
  90.7 4.1 %all-to-all-start.4 = ((bf16[4,64,1536]{2,1,0:T(8,128)(2,1)}), bf16[4,64,1536]{2,1,0:T(8,128)(2,1)S(1)}, u32[]{:S(2)}, u32[]{:S(2)}) async-start(bf16[4,64,1536]{2,1,0:T(8,128)(2,1)} %bitcast.1), calls=%async_computation.4 | async-start | bytes 1572864 | tf_op jit(solution)/shard_map/sum_a_z/all_to_all | solution.py:358
  94.7 2.9 %collective-permute-start.6 = (bf16[64,1536]{1,0:T(8,128)(2,1)S(1)}, bf16[64,1536]{1,0:T(8,128)(2,1)S(1)}, u32[]{:S(2)}, u32[]{:S(2)}) collective-permute-start(bf16[64,1536]{1,0:T(8,128)(2,1)S(1)} %get-tuple-element.20), channel_id=1, source_target_pairs={{0,2},{2,0},{1,3},{3,1},{4,6},{6,4},{5,7},{7,5},{8,10},{10,8},{9,1... | collective-permute-start | bytes 589832 | tf_op jit(solution)/shard_map/sum_b_y/ppermute | solution.py:38
  98.4 5.4 %collective-permute-done.6.refs_1_ = bf16[64,1536]{1,0:T(8,128)(2,1)S(1)} collective-permute-done((bf16[64,1536]{1,0:T(8,128)(2,1)S(1)}, bf16[64,1536]{1,0:T(8,128)(2,1)S(1)}, u32[]{:S(2)}, u32[]{:S(2)}) %collective-permute-start.6) | collective-permute-done | bytes 196640 | tf_op jit(solution)/shard_map/sum_b_y/ppermute | solution.py:38
  103.9 2.9 %all-to-all-done.4.refs_0_ = bf16[4,64,1536]{2,1,0:T(8,128)(2,1)S(1)} async-done(((bf16[4,64,1536]{2,1,0:T(8,128)(2,1)}), bf16[4,64,1536]{2,1,0:T(8,128)(2,1)S(1)}, u32[]{:S(2)}, u32[]{:S(2)}) %all-to-all-start.4) | async-done | bytes 786464 | tf_op jit(solution)/shard_map/sum_a_z/all_to_all | solution.py:358
  107.9 4.2 %all-to-all-start.5 = ((bf16[4,64,1536]{2,1,0:T(8,128)(2,1)}), bf16[4,64,1536]{2,1,0:T(8,128)(2,1)}, u32[]{:S(2)}, u32[]{:S(2)}) async-start(bf16[4,64,1536]{2,1,0:T(8,128)(2,1)} %finish_a.1.refs_2_), calls=%async_computation.5 | async-start | bytes 1572864 | tf_op jit(solution)/shard_map/all_a_z/all_to_all | solution.py:358
  112.1 7.1 %collective-permute-done.10.refs_1_ = bf16[256,1536]{1,0:T(8,128)(2,1)S(1)} collective-permute-done((bf16[256,1536]{1,0:T(8,128)(2,1)}, bf16[256,1536]{1,0:T(8,128)(2,1)S(1)}, u32[]{:S(2)}, u32[]{:S(2)}) %collective-permute-start.10) | collective-permute-done | bytes 786464 | tf_op jit(solution)/shard_map/sum_cot_y/ppermute | solution.py:38
  120.3 3.0 %all-to-all-done.5 = bf16[4,64,1536]{2,1,0:T(8,128)(2,1)} async-done(((bf16[4,64,1536]{2,1,0:T(8,128)(2,1)}), bf16[4,64,1536]{2,1,0:T(8,128)(2,1)}, u32[]{:S(2)}, u32[]{:S(2)}) %all-to-all-start.5) | async-done | bytes 786464 | tf_op jit(solution)/shard_map/all_a_z/all_to_all | solution.py:358
  123.4 3.5 %all-to-all-start.6 = ((bf16[4,64,1536]{2,1,0:T(8,128)(2,1)}), bf16[4,64,1536]{2,1,0:T(8,128)(2,1)S(1)}, u32[]{:S(2)}, u32[]{:S(2)}) async-start(bf16[4,64,1536]{2,1,0:T(8,128)(2,1)} %bitcast.3), calls=%async_computation.6 | async-start | bytes 1572864 | tf_op jit(solution)/shard_map/sum_cot_z/all_to_all | solution.py:358
  126.9 3.0 %collective-permute-start.7 = (bf16[256,1536]{1,0:T(8,128)(2,1)}, bf16[256,1536]{1,0:T(8,128)(2,1)}, u32[]{:S(2)}, u32[]{:S(2)}) collective-permute-start(bf16[256,1536]{1,0:T(8,128)(2,1)} %bitcast.2.refs_0_), channel_id=1, source_target_pairs={{0,2},{2,0},{1,3},{3,1},{4,6},{6,4},{5,7},{7,5},{8,10},{10,8},{9,1... | collective-permute-start | bytes 2359304 | tf_op jit(solution)/shard_map/all_a_y/ppermute | solution.py:38
  129.9 6.9 %all-to-all-done.6.refs_0_ = bf16[4,64,1536]{2,1,0:T(8,128)(2,1)S(1)} async-done(((bf16[4,64,1536]{2,1,0:T(8,128)(2,1)}), bf16[4,64,1536]{2,1,0:T(8,128)(2,1)S(1)}, u32[]{:S(2)}, u32[]{:S(2)}) %all-to-all-start.6) | async-done | bytes 786464 | tf_op jit(solution)/shard_map/sum_cot_z/all_to_all | solution.py:358
  136.8 1.2 finish_back.1.refs_5_
  138.0 4.2 %all-to-all-start.8 = ((bf16[4,64,1536]{2,1,0:T(8,128)(2,1)}), bf16[4,64,1536]{2,1,0:T(8,128)(2,1)}, u32[]{:S(2)}, u32[]{:S(2)}) async-start(bf16[4,64,1536]{2,1,0:T(8,128)(2,1)} %finish_back.1.refs_5_), calls=%async_computation.8 | async-start | bytes 1572864 | tf_op jit(solution)/shard_map/all_back_z/all_to_all | solution.py:358
  142.2 3.0 %collective-permute-start.14 = (bf16[64,1536]{1,0:T(8,128)(2,1)S(1)}, bf16[64,1536]{1,0:T(8,128)(2,1)S(1)}, u32[]{:S(2)}, u32[]{:S(2)}) collective-permute-start(bf16[64,1536]{1,0:T(8,128)(2,1)S(1)} %get-tuple-element.23.refs_0_), channel_id=1, source_target_pairs={{0,2},{2,0},{1,3},{3,1},{4,6},{6,4},{5,7},{7,5},{8,10},{10,8},{9,1... | collective-permute-start | bytes 589832 | tf_op jit(solution)/shard_map/all_b_y/ppermute | solution.py:38
  145.2 4.4 %collective-permute-done.14.refs_1_ = bf16[64,1536]{1,0:T(8,128)(2,1)S(1)} collective-permute-done((bf16[64,1536]{1,0:T(8,128)(2,1)S(1)}, bf16[64,1536]{1,0:T(8,128)(2,1)S(1)}, u32[]{:S(2)}, u32[]{:S(2)}) %collective-permute-start.14) | collective-permute-done | bytes 196640 | tf_op jit(solution)/shard_map/all_b_y/ppermute | solution.py:38
  149.6 2.2 all-to-all-done.8
  151.9 1.1 copy-done.15
  153.0 3.6 %all-to-all-start.9 = ((bf16[4,2,64,1536]{3,2,1,0:T(8,128)(2,1)}), bf16[4,2,64,1536]{3,2,1,0:T(8,128)(2,1)S(1)}, u32[]{:S(2)}, u32[]{:S(2)}) async-start(bf16[4,2,64,1536]{3,2,1,0:T(8,128)(2,1)} %copy-done.15), calls=%async_computation.9 | async-start | bytes 3145728 | tf_op jit(solution)/shard_map/all_b_z/all_to_all | solution.py:358
  157.2 2.9 %collective-permute-start.11 = (bf16[256,1536]{1,0:T(8,128)(2,1)}, bf16[256,1536]{1,0:T(8,128)(2,1)S(1)}, u32[]{:S(2)}, u32[]{:S(2)}) collective-permute-start(bf16[256,1536]{1,0:T(8,128)(2,1)} %bitcast.5.refs_3_.refs_0_.refs_1_), channel_id=1, source_target_pairs={{0,2},{2,0},{1,3},{3,1},{4,6},{6,4},{5,7},{7,5},{8,10},{10,8},{9,1... | collective-permute-start | bytes 2359304 | tf_op jit(solution)/shard_map/all_back_y/ppermute | solution.py:38
  160.4 7.1 %down.2.refs_1_.refs_3_ = bf16[8,2,32,768]{3,2,1,0:T(8,128)(2,1)} custom-call(s32[1]{0:T(128)} %bitcast.core, bf16[256,1536]{1,0:T(8,128)(2,1)} %bitcast.2.refs_0_, bf16[256,1536]{1,0:T(8,128)(2,1)} %collective-permute-done.7.refs_1_.refs_2_, bf16[256,1536]{1,0:T(8,128)(2,1)} %collective-permute-done.8.refs_2_, ...), custom_call_target="tpu_custom_call" | custom-call | bytes 18000 | tf_op jit(solution)/shard_map/down/pallas_call | solution.py:65
  167.5 10.9 %collective-permute-done.11.refs_0_.refs_2_.refs_1_ = bf16[256,1536]{1,0:T(8,128)(2,1)S(1)} collective-permute-done((bf16[256,1536]{1,0:T(8,128)(2,1)}, bf16[256,1536]{1,0:T(8,128)(2,1)S(1)}, u32[]{:S(2)}, u32[]{:S(2)}) %collective-permute-start.11) | collective-permute-done | bytes 786464 | tf_op jit(solution)/shard_map/all_back_y/ppermute | solution.py:38
  178.4 1.2 relay.7
  181.1 1.1 copy-done.8
  183.2 4.4 %all-to-all-start.7 = ((bf16[8,2,32,768]{3,2,1,0:T(8,128)(2,1)}), bf16[8,2,32,768]{3,2,1,0:T(8,128)(2,1)}, u32[]{:S(2)}, u32[]{:S(2)}) async-start(bf16[8,2,32,768]{3,2,1,0:T(8,128)(2,1)} %down.2.refs_1_.refs_3_), calls=%async_computation.7 | async-start | bytes 1572864 | tf_op jit(solution)/shard_map/row_out/all_to_all | solution.py:120
  187.6 6.8 %grad.2.refs_5_ = bf16[3072,768]{1,0:T(8,128)(2,1)} custom-call(s32[1]{0:T(128)} %bitcast.core, bf16[8,2,32,768]{3,2,1,0:T(8,128)(2,1)S(1)} %copy-done.3, bf16[4,2,64,1536]{3,2,1,0:T(8,128)(2,1)S(1)} %all-to-all-done.9.refs_0_.refs_1_, bf16[4,2,64,1536]{3,2,1,0:T(8,128)(2,1)} %collective-permute-done.15.refs_2_, bf16[8,2,32,768]{3,2,1,0:T(8,128)(2,1)} %down.2.refs_1_.refs_3_), custom_call_target="tpu_custom_call" | custom-call | bytes 18000 | tf_op jit(solution)/shard_map/grad/pallas_call | solution.py:65
  194.5 7.2 %down.3.refs_5_ = bf16[8,2,32,768]{3,2,1,0:T(8,128)(2,1)} custom-call(s32[1]{0:T(128)} %bitcast.core, bf16[256,1536]{1,0:T(8,128)(2,1)} %bitcast.5.refs_3_.refs_0_.refs_1_, bf16[256,1536]{1,0:T(8,128)(2,1)} %copy-done.7, bf16[256,1536]{1,0:T(8,128)(2,1)} %collective-permute-done.12.refs_2_.refs_3_, ...), custom_call_target="tpu_custom_call" | custom-call | bytes 18000 | tf_op jit(solution)/shard_map/down/pallas_call | solution.py:65
  201.7 5.6 %all-to-all-start.10 = ((bf16[8,2,32,768]{3,2,1,0:T(8,128)(2,1)}), bf16[8,2,32,768]{3,2,1,0:T(8,128)(2,1)}, u32[]{:S(2)}, u32[]{:S(2)}) async-start(bf16[8,2,32,768]{3,2,1,0:T(8,128)(2,1)} %down.3.refs_5_), calls=%async_computation.10 | async-start | bytes 1572864 | tf_op jit(solution)/shard_map/row_in/all_to_all | solution.py:120
  208.0 1.9 settle_kernel.2
  209.9 1.1 copy-done.14
  211.0 7.0 %grad.3 = (bf16[768,3072]{1,0:T(8,128)(2,1)}, f32[1,3072]{1,0:T(1,128)}) custom-call(s32[1]{0:T(128)} %bitcast.core, bf16[8,2,32,768]{3,2,1,0:T(8,128)(2,1)S(1)} %copy-done.6, bf16[256,1536]{1,0:T(8,128)(2,1)} %bitcast.5.refs_3_.refs_0_.refs_1_, bf16[256,1536]{1,0:T(8,128)(2,1)S(1)} %copy-done.9, bf16[256,1536]{1,0:T(8,128)(2,1)} %collective-permute-done.12.refs_2_.refs_3_, ...), custom_call_target="tpu_custom_call" | custom-call | bytes 18000 | tf_op jit(solution)/shard_map/grad/pallas_call | solution.py:65
  218.1 2.2 all-to-all-done.10
  220.2 1.9 settle_kernel.3
  (85 shorter events, 15.0 us)
Async XLA Ops:
  19.3 2.3 %copy-start = (bf16[768,3072]{1,0:T(8,128)(2,1)S(1)}, bf16[768,3072]{1,0:T(8,128)(2,1)}, u32[]{:S(2)}) copy-start(bf16[768,3072]{1,0:T(8,128)(2,1)} %refs_4_.3) | copy-start | bytes 14155780
  21.7 2.1 copy-start.13
  21.7 2.6 %copy-start.19 = (bf16[64,768]{1,0:T(8,128)(2,1)S(1)}, bf16[64,768]{1,0:T(8,128)(2,1)}, u32[]{:S(2)}) copy-start(bf16[64,768]{1,0:T(8,128)(2,1)} %refs_0_.7) | copy-start | bytes 294916
  23.7 6.0 %collective-permute-start.1 = (bf16[768,1536]{1,0:T(8,128)(2,1)}, bf16[768,1536]{1,0:T(8,128)(2,1)}, u32[]{:S(2)}, u32[]{:S(2)}) collective-permute-start(bf16[768,1536]{1,0:T(8,128)(2,1)} %exchanged.2), channel_id=1, source_target_pairs={{0,1},{1,0},{2,3},{3,2},{4,5},{5,4},{6,7},{7,6},{8,9},{9,8},{10,11... | collective-permute-start | bytes 7077896 | tf_op jit(solution)/shard_map/core_swap/ppermute | solution.py:38
  23.7 5.3 %collective-permute-start = (bf16[8,2,32,768]{3,2,1,0:T(8,128)(2,1)S(1)}, bf16[8,2,32,768]{3,2,1,0:T(8,128)(2,1)S(1)}, u32[]{:S(2)}, u32[]{:S(2)}) collective-permute-start(bf16[8,2,32,768]{3,2,1,0:T(8,128)(2,1)S(1)} %all_to_all.55.refs_1_.refs_0_), channel_id=1, source_target_pairs={{0,1},{1,0},{2,3},{3,2},{4,5},{5,4},{6,7},{7,6},{8,9},{9,8},{10,11... | collective-permute-start | bytes 2359304 | tf_op jit(solution)/shard_map/core_swap/ppermute | solution.py:38
  25.2 17.3 %all-to-all-start.1 = ((bf16[8,2,32,768]{3,2,1,0:T(8,128)(2,1)}), bf16[8,2,32,768]{3,2,1,0:T(8,128)(2,1)S(1)}, u32[]{:S(2)}, u32[]{:S(2)}) async-start(bf16[8,2,32,768]{3,2,1,0:T(8,128)(2,1)} %spread_kernel.4), calls=%async_computation.1 | async-start | bytes 1572864 | tf_op jit(solution)/shard_map/row_b/all_to_all | solution.py:94
  29.0 0.9 copy-start.21
  36.8 2.3 %copy-start.1 = (bf16[3072,768]{1,0:T(8,128)(2,1)S(1)}, bf16[3072,768]{1,0:T(8,128)(2,1)}, u32[]{:S(2)}) copy-start(bf16[3072,768]{1,0:T(8,128)(2,1)} %refs_4_.2) | copy-start | bytes 14155780
  39.1 1.1 copy-start.10
  40.2 2.2 %copy-start.11 = (bf16[256,1536]{1,0:T(8,128)(2,1)S(1)}, bf16[256,1536]{1,0:T(8,128)(2,1)}, u32[]{:S(2)}) copy-start(bf16[256,1536]{1,0:T(8,128)(2,1)} %get-tuple-element.16.refs_1_.refs_0_) | copy-start | bytes 2359300
  42.1 28.1 %collective-permute-start.5 = (bf16[1536,768]{1,0:T(8,128)(2,1)}, bf16[1536,768]{1,0:T(8,128)(2,1)}, u32[]{:S(2)}, u32[]{:S(2)}) collective-permute-start(bf16[1536,768]{1,0:T(8,128)(2,1)} %exchanged.3), channel_id=1, source_target_pairs={{0,1},{1,0},{2,3},{3,2},{4,5},{5,4},{6,7},{7,6},{8,9},{9,8},{10,11... | collective-permute-start | bytes 7077896 | tf_op jit(solution)/shard_map/core_swap/ppermute | solution.py:38
  42.5 1.5 copy-start.5
  42.5 6.8 %collective-permute-start.3 = (bf16[8,2,32,768]{3,2,1,0:T(8,128)(2,1)S(1)}, bf16[8,2,32,768]{3,2,1,0:T(8,128)(2,1)}, u32[]{:S(2)}, u32[]{:S(2)}) collective-permute-start(bf16[8,2,32,768]{3,2,1,0:T(8,128)(2,1)S(1)} %relay.4), channel_id=1, source_target_pairs={{0,1},{1,0},{2,3},{3,2},{4,5},{5,4},{6,7},{7,6},{8,9},{9,8},{10,11... | collective-permute-start | bytes 2359304 | tf_op jit(solution)/shard_map/core_swap/ppermute | solution.py:38
  44.0 17.7 %all-to-all-start.3 = ((bf16[8,2,32,768]{3,2,1,0:T(8,128)(2,1)}), bf16[8,2,32,768]{3,2,1,0:T(8,128)(2,1)S(1)}, u32[]{:S(2)}, u32[]{:S(2)}) async-start(bf16[8,2,32,768]{3,2,1,0:T(8,128)(2,1)} %spread_kernel.5), calls=%async_computation.3 | async-start | bytes 1572864 | tf_op jit(solution)/shard_map/row_cot/all_to_all | solution.py:94
  56.3 10.8 %copy-start.4 = (bf16[4,2,64,1536]{3,2,1,0:T(8,128)(2,1)S(1)}, bf16[4,2,64,1536]{3,2,1,0:T(8,128)(2,1)}, u32[]{:S(2)}) copy-start(bf16[4,2,64,1536]{3,2,1,0:T(8,128)(2,1)} %up.4.refs_1_) | copy-start | bytes 4718596
  61.7 5.4 %copy-start.2 = (bf16[8,2,32,768]{3,2,1,0:T(8,128)(2,1)}, bf16[8,2,32,768]{3,2,1,0:T(8,128)(2,1)S(1)}, u32[]{:S(2)}) copy-start(bf16[8,2,32,768]{3,2,1,0:T(8,128)(2,1)S(1)} %all-to-all-done.3.refs_0_) | copy-start | bytes 2359300
  61.7 25.1 %all-to-all-start.2 = ((bf16[4,2,64,1536]{3,2,1,0:T(8,128)(2,1)}), bf16[4,2,64,1536]{3,2,1,0:T(8,128)(2,1)}, u32[]{:S(2)}, u32[]{:S(2)}) async-start(bf16[4,2,64,1536]{3,2,1,0:T(8,128)(2,1)} %up.4.refs_1_), calls=%async_computation.2 | async-start | bytes 3145728 | tf_op jit(solution)/shard_map/sum_b_z/all_to_all | solution.py:358
  67.1 3.1 %collective-permute-start.4 = (bf16[8,2,32,768]{3,2,1,0:T(8,128)(2,1)S(1)}, bf16[8,2,32,768]{3,2,1,0:T(8,128)(2,1)S(1)}, u32[]{:S(2)}, u32[]{:S(2)}) collective-permute-start(bf16[8,2,32,768]{3,2,1,0:T(8,128)(2,1)S(1)} %relay.5), channel_id=1, source_target_pairs={{0,1},{1,0},{2,3},{3,2},{4,5},{5,4},{6,7},{7,6},{8,9},{9,8},{10,11... | collective-permute-start | bytes 2359304 | tf_op jit(solution)/shard_map/core_swap/ppermute | solution.py:38
  67.2 22.4 %collective-permute-start.2 = (bf16[256,1536]{1,0:T(8,128)(2,1)}, bf16[256,1536]{1,0:T(8,128)(2,1)S(1)}, u32[]{:S(2)}, u32[]{:S(2)}) collective-permute-start(bf16[256,1536]{1,0:T(8,128)(2,1)} %get-tuple-element.17), channel_id=1, source_target_pairs={{0,2},{2,0},{1,3},{3,1},{4,6},{6,4},{5,7},{7,5},{8,10},{10,8},{9,1... | collective-permute-start | bytes 2359304 | tf_op jit(solution)/shard_map/sum_a_y/ppermute | solution.py:38
  70.2 1.0 copy-start.22
  78.3 11.3 %copy-start.12 = (bf16[256,1536]{1,0:T(8,128)(2,1)S(1)}, bf16[256,1536]{1,0:T(8,128)(2,1)}, u32[]{:S(2)}) copy-start(bf16[256,1536]{1,0:T(8,128)(2,1)} %get-tuple-element.16.refs_1_.refs_0_) | copy-start | bytes 2359300
  86.9 1.1 copy-start.16
  89.6 8.7 %copy-start.23 = (f32[3072]{0:T(1024)S(1)}, f32[3072]{0:T(1024)}, u32[]{:S(2)}) copy-start(f32[3072]{0:T(1024)} %param.11) | copy-start | bytes 36868
  90.7 16.2 %all-to-all-start.4 = ((bf16[4,64,1536]{2,1,0:T(8,128)(2,1)}), bf16[4,64,1536]{2,1,0:T(8,128)(2,1)S(1)}, u32[]{:S(2)}, u32[]{:S(2)}) async-start(bf16[4,64,1536]{2,1,0:T(8,128)(2,1)} %bitcast.1), calls=%async_computation.4 | async-start | bytes 1572864 | tf_op jit(solution)/shard_map/sum_a_z/all_to_all | solution.py:358
  94.7 24.5 %copy-start.17 = (bf16[256,1536]{1,0:T(8,128)(2,1)S(1)}, bf16[256,1536]{1,0:T(8,128)(2,1)}, u32[]{:S(2)}) copy-start(bf16[256,1536]{1,0:T(8,128)(2,1)} %get-tuple-element.18.refs_1_.refs_0_) | copy-start | bytes 2359300
  94.7 9.0 %collective-permute-start.6 = (bf16[64,1536]{1,0:T(8,128)(2,1)S(1)}, bf16[64,1536]{1,0:T(8,128)(2,1)S(1)}, u32[]{:S(2)}, u32[]{:S(2)}) collective-permute-start(bf16[64,1536]{1,0:T(8,128)(2,1)S(1)} %get-tuple-element.20), channel_id=1, source_target_pairs={{0,2},{2,0},{1,3},{3,1},{4,6},{6,4},{5,7},{7,5},{8,10},{10,8},{9,1... | collective-permute-start | bytes 589832 | tf_op jit(solution)/shard_map/sum_b_y/ppermute | solution.py:38
  97.6 21.6 %collective-permute-start.10 = (bf16[256,1536]{1,0:T(8,128)(2,1)}, bf16[256,1536]{1,0:T(8,128)(2,1)S(1)}, u32[]{:S(2)}, u32[]{:S(2)}) collective-permute-start(bf16[256,1536]{1,0:T(8,128)(2,1)} %get-tuple-element.22), channel_id=1, source_target_pairs={{0,2},{2,0},{1,3},{3,1},{4,6},{6,4},{5,7},{7,5},{8,10},{10,8},{9,1... | collective-permute-start | bytes 2359304 | tf_op jit(solution)/shard_map/sum_cot_y/ppermute | solution.py:38
  107.9 15.4 %all-to-all-start.5 = ((bf16[4,64,1536]{2,1,0:T(8,128)(2,1)}), bf16[4,64,1536]{2,1,0:T(8,128)(2,1)}, u32[]{:S(2)}, u32[]{:S(2)}) async-start(bf16[4,64,1536]{2,1,0:T(8,128)(2,1)} %finish_a.1.refs_2_), calls=%async_computation.5 | async-start | bytes 1572864 | tf_op jit(solution)/shard_map/all_a_z/all_to_all | solution.py:358
  123.4 13.4 %all-to-all-start.6 = ((bf16[4,64,1536]{2,1,0:T(8,128)(2,1)}), bf16[4,64,1536]{2,1,0:T(8,128)(2,1)S(1)}, u32[]{:S(2)}, u32[]{:S(2)}) async-start(bf16[4,64,1536]{2,1,0:T(8,128)(2,1)} %bitcast.3), calls=%async_computation.6 | async-start | bytes 1572864 | tf_op jit(solution)/shard_map/sum_cot_z/all_to_all | solution.py:358
  126.9 22.7 %collective-permute-start.7 = (bf16[256,1536]{1,0:T(8,128)(2,1)}, bf16[256,1536]{1,0:T(8,128)(2,1)}, u32[]{:S(2)}, u32[]{:S(2)}) collective-permute-start(bf16[256,1536]{1,0:T(8,128)(2,1)} %bitcast.2.refs_0_), channel_id=1, source_target_pairs={{0,2},{2,0},{1,3},{3,1},{4,6},{6,4},{5,7},{7,5},{8,10},{10,8},{9,1... | collective-permute-start | bytes 2359304 | tf_op jit(solution)/shard_map/all_a_y/ppermute | solution.py:38
  138.0 13.7 %all-to-all-start.8 = ((bf16[4,64,1536]{2,1,0:T(8,128)(2,1)}), bf16[4,64,1536]{2,1,0:T(8,128)(2,1)}, u32[]{:S(2)}, u32[]{:S(2)}) async-start(bf16[4,64,1536]{2,1,0:T(8,128)(2,1)} %finish_back.1.refs_5_), calls=%async_computation.8 | async-start | bytes 1572864 | tf_op jit(solution)/shard_map/all_back_z/all_to_all | solution.py:358
  142.2 7.3 %collective-permute-start.14 = (bf16[64,1536]{1,0:T(8,128)(2,1)S(1)}, bf16[64,1536]{1,0:T(8,128)(2,1)S(1)}, u32[]{:S(2)}, u32[]{:S(2)}) collective-permute-start(bf16[64,1536]{1,0:T(8,128)(2,1)S(1)} %get-tuple-element.23.refs_0_), channel_id=1, source_target_pairs={{0,2},{2,0},{1,3},{3,1},{4,6},{6,4},{5,7},{7,5},{8,10},{10,8},{9,1... | collective-permute-start | bytes 589832 | tf_op jit(solution)/shard_map/all_b_y/ppermute | solution.py:38
  151.9 1.1 copy-start.15
  153.0 25.4 %all-to-all-start.9 = ((bf16[4,2,64,1536]{3,2,1,0:T(8,128)(2,1)}), bf16[4,2,64,1536]{3,2,1,0:T(8,128)(2,1)S(1)}, u32[]{:S(2)}, u32[]{:S(2)}) async-start(bf16[4,2,64,1536]{3,2,1,0:T(8,128)(2,1)} %copy-done.15), calls=%async_computation.9 | async-start | bytes 3145728 | tf_op jit(solution)/shard_map/all_b_z/all_to_all | solution.py:358
  156.6 3.5 %collective-permute-start.8 = (bf16[256,1536]{1,0:T(8,128)(2,1)}, bf16[256,1536]{1,0:T(8,128)(2,1)}, u32[]{:S(2)}, u32[]{:S(2)}) collective-permute-start(bf16[256,1536]{1,0:T(8,128)(2,1)} %bitcast.2.refs_0_), channel_id=1, source_target_pairs={{0,1},{1,0},{2,3},{3,2},{4,5},{5,4},{6,7},{7,6},{8,9},{9,8},{10,11... | collective-permute-start | bytes 2359304 | tf_op jit(solution)/shard_map/core_swap/ppermute | solution.py:38
  156.7 3.7 %collective-permute-start.9 = (bf16[256,1536]{1,0:T(8,128)(2,1)}, bf16[256,1536]{1,0:T(8,128)(2,1)}, u32[]{:S(2)}, u32[]{:S(2)}) collective-permute-start(bf16[256,1536]{1,0:T(8,128)(2,1)} %collective-permute-done.7.refs_1_.refs_2_), channel_id=1, source_target_pairs={{0,1},{1,0},{2,3},{3,2},{4,5},{5,4},{6,7},{7,6},{8,9},{9,8},{10,11... | collective-permute-start | bytes 2359304 | tf_op jit(solution)/shard_map/core_swap/ppermute | solution.py:38
  157.2 21.3 %collective-permute-start.11 = (bf16[256,1536]{1,0:T(8,128)(2,1)}, bf16[256,1536]{1,0:T(8,128)(2,1)S(1)}, u32[]{:S(2)}, u32[]{:S(2)}) collective-permute-start(bf16[256,1536]{1,0:T(8,128)(2,1)} %bitcast.5.refs_3_.refs_0_.refs_1_), channel_id=1, source_target_pairs={{0,2},{2,0},{1,3},{3,1},{4,6},{6,4},{5,7},{7,5},{8,10},{10,8},{9,1... | collective-permute-start | bytes 2359304 | tf_op jit(solution)/shard_map/all_back_y/ppermute | solution.py:38
  180.6 7.1 %copy-start.3 = (bf16[8,2,32,768]{3,2,1,0:T(8,128)(2,1)S(1)}, bf16[8,2,32,768]{3,2,1,0:T(8,128)(2,1)}, u32[]{:S(2)}) copy-start(bf16[8,2,32,768]{3,2,1,0:T(8,128)(2,1)} %copy-done.2) | copy-start | bytes 2359300
  180.6 7.1 %collective-permute-start.15 = (bf16[4,2,64,1536]{3,2,1,0:T(8,128)(2,1)}, bf16[4,2,64,1536]{3,2,1,0:T(8,128)(2,1)}, u32[]{:S(2)}, u32[]{:S(2)}) collective-permute-start(bf16[4,2,64,1536]{3,2,1,0:T(8,128)(2,1)} %relay.7), channel_id=1, source_target_pairs={{0,1},{1,0},{2,3},{3,2},{4,5},{5,4},{6,7},{7,6},{8,9},{9,8},{10,11... | collective-permute-start | bytes 4718600 | tf_op jit(solution)/shard_map/core_swap/ppermute | solution.py:38
  180.6 13.9 %collective-permute-start.12 = (bf16[256,1536]{1,0:T(8,128)(2,1)}, bf16[256,1536]{1,0:T(8,128)(2,1)}, u32[]{:S(2)}, u32[]{:S(2)}) collective-permute-start(bf16[256,1536]{1,0:T(8,128)(2,1)} %bitcast.5.refs_3_.refs_0_.refs_1_), channel_id=1, source_target_pairs={{0,1},{1,0},{2,3},{3,2},{4,5},{5,4},{6,7},{7,6},{8,9},{9,8},{10,11... | collective-permute-start | bytes 2359304 | tf_op jit(solution)/shard_map/core_swap/ppermute | solution.py:38
  181.1 1.1 copy-start.8
  183.2 11.3 %collective-permute-start.13 = (bf16[256,1536]{1,0:T(8,128)(2,1)}, bf16[256,1536]{1,0:T(8,128)(2,1)}, u32[]{:S(2)}, u32[]{:S(2)}) collective-permute-start(bf16[256,1536]{1,0:T(8,128)(2,1)} %relay.6), channel_id=1, source_target_pairs={{0,1},{1,0},{2,3},{3,2},{4,5},{5,4},{6,7},{7,6},{8,9},{9,8},{10,11... | collective-permute-start | bytes 2359304 | tf_op jit(solution)/shard_map/core_swap/ppermute | solution.py:38
  183.2 18.5 %all-to-all-start.7 = ((bf16[8,2,32,768]{3,2,1,0:T(8,128)(2,1)}), bf16[8,2,32,768]{3,2,1,0:T(8,128)(2,1)}, u32[]{:S(2)}, u32[]{:S(2)}) async-start(bf16[8,2,32,768]{3,2,1,0:T(8,128)(2,1)} %down.2.refs_1_.refs_3_), calls=%async_computation.7 | async-start | bytes 1572864 | tf_op jit(solution)/shard_map/row_out/all_to_all | solution.py:120
  194.5 12.8 %copy-start.24 = (f32[768]{0:T(1024)S(1)}, f32[768]{0:T(1024)}, u32[]{:S(2)}) copy-start(f32[768]{0:T(1024)} %param.13) | copy-start | bytes 9220
  201.7 8.2 %copy-start.6 = (bf16[8,2,32,768]{3,2,1,0:T(8,128)(2,1)S(1)}, bf16[8,2,32,768]{3,2,1,0:T(8,128)(2,1)}, u32[]{:S(2)}) copy-start(bf16[8,2,32,768]{3,2,1,0:T(8,128)(2,1)} %copy-done.5) | copy-start | bytes 2359300
  201.7 8.2 %copy-start.9 = (bf16[256,1536]{1,0:T(8,128)(2,1)S(1)}, bf16[256,1536]{1,0:T(8,128)(2,1)}, u32[]{:S(2)}) copy-start(bf16[256,1536]{1,0:T(8,128)(2,1)} %copy-done.7) | copy-start | bytes 2359300
  201.7 18.5 %all-to-all-start.10 = ((bf16[8,2,32,768]{3,2,1,0:T(8,128)(2,1)}), bf16[8,2,32,768]{3,2,1,0:T(8,128)(2,1)}, u32[]{:S(2)}, u32[]{:S(2)}) async-start(bf16[8,2,32,768]{3,2,1,0:T(8,128)(2,1)} %down.3.refs_5_), calls=%async_computation.10 | async-start | bytes 1572864 | tf_op jit(solution)/shard_map/row_in/all_to_all | solution.py:120
  209.9 1.1 copy-start.14
  (3 other events, 2.7 us)

commit v3 on v2

--- a/solution.py
+++ b/solution.py
@@ -19,7 +19,7 @@
 VMEM_LIMIT = 40 << 20
 ALL_VMEM = 61 << 20
 MICRO = 3_000
-TILE = 512
+TILE = 768
 
 
 def gelu_tanh(values):
@@ -346,6 +346,14 @@
     return simple(body, [near, far], [like((copies, 2) + near.shape)], waits)[0]
 
 
+def copied(values, copies, waits):
+    def body(x, out):
+        for i in range(copies):
+            out[i] = x[...]
+
+    return simple(body, [values], [like((copies,) + values.shape)], waits)[0]
+
+
 def relay(values, waits):
     def body(x, out):
         out[...] = x[...]

time: 224 us -> 222 us (level)
  Pallas kernels: 67.3 us -> 64.9 us
    pallas_call x25, Pallas kernels: 67.3 us -> 64.9 us  [call(): pl.pallas_call(kernel, name=name, grid_spec=pltpu.PrefetchScalarGridSpec(...]
  transfers between devices with their start and end apart: 26 -> 26, of which waited for: 14 -> 15; matrix products, arithmetic and copies ran while one was open for 0% -> 0% of each run, Pallas kernels for 27% -> 27%
where the time goes in v3:
time: 222 us; the launch traced here: 221 us
  Pallas kernels  64.9 us (29%)
  waiting for transfers between devices  62.2 us (28%)
  starting transfers between devices  60.7 us (27%)
  blocking collectives  17.7 us (8%)
  local copies, waits for them, and re-layouts  13.7 us (6%)
    pallas_call x25, Pallas kernels, call(): pl.pallas_call(kernel, name=name, grid_spec=pltpu.PrefetchScalarGridSpec(...  64.9 us
    ppermute x16, waiting for transfers between devices, swap(): return lax.ppermute(values, axis, [(0, 1), (1, 0)])  29.1 us
    all_to_all x6, starting transfers between devices, along_z(): return lax.all_to_all(values, 'z', 0, 0)  24.8 us
    all_to_all x6, waiting for transfers between devices, along_z(): return lax.all_to_all(values, 'z', 0, 0)  24 us
    all_to_all x1, blocking collectives, tokens_of(): return (lax.all_to_all(copies, ROW, 0, 0), copies)  17.7 us
    ppermute x16, starting transfers between devices, swap(): return lax.ppermute(values, axis, [(0, 1), (1, 0)])  17.6 us
    unnamed x50, local copies, waits for them, and re-layouts  13.6 us
    all_to_all x2, starting transfers between devices, sum_hidden(): got = lax.all_to_all(parts, ROW, 0, 0).reshape(rows, subs * sub, width)  9.32 us
  transfers between devices with their start and end apart: 26, of which 15 were waited for; matrix products, arithmetic and copies ran while one was open for 0% of the time, Pallas kernels for 27%

profile of v3, /device:TPU:0, one launch (start us, length us, event | category | flops | bytes accessed | tf_op | source)
XLA Modules:
  0.0 220.8 jit_solution(9170901416149828838)
XLA Ops:
  1.6 17.7 %all_to_all.55.refs_1_.refs_0_ = bf16[8,2,32,768]{3,2,1,0:T(8,128)(2,1)S(1)} all-to-all(bf16[8,2,32,768]{3,2,1,0:T(8,128)(2,1)S(1)} %spread_kernel.3), channel_id=1, replica_groups=mesh['x'=4,'yl'=2,'z'=4,'yh'=2,'core'=2] {'x','yl'}, dimensions={0} | all-to-all | bytes 1572864 | tf_op jit(solution)/shard_map/row_a/all_to_all | solution.py:94
  19.3 2.3 %copy-done = bf16[768,3072]{1,0:T(8,128)(2,1)S(1)} copy-done((bf16[768,3072]{1,0:T(8,128)(2,1)S(1)}, bf16[768,3072]{1,0:T(8,128)(2,1)}, u32[]{:S(2)}) %copy-start) | copy-done | bytes 4718616
  21.7 1.7 exchanged.2
  24.8 3.5 %all-to-all-start.1 = ((bf16[8,2,32,768]{3,2,1,0:T(8,128)(2,1)}), bf16[8,2,32,768]{3,2,1,0:T(8,128)(2,1)S(1)}, u32[]{:S(2)}, u32[]{:S(2)}) async-start(bf16[8,2,32,768]{3,2,1,0:T(8,128)(2,1)} %spread_kernel.4), calls=%async_computation.1 | async-start | bytes 1572864 | tf_op jit(solution)/shard_map/row_b/all_to_all | solution.py:94
  29.6 6.7 %up.3 = (bf16[256,1536]{1,0:T(8,128)(2,1)}, bf16[256,1536]{1,0:T(8,128)(2,1)}) custom-call(s32[1]{0:T(128)} %bitcast.core, bf16[8,2,32,768]{3,2,1,0:T(8,128)(2,1)} %copy-done.13, bf16[8,2,32,768]{3,2,1,0:T(8,128)(2,1)} %copy-done.21, bf16[768,3072]{1,0:T(8,128)(2,1)} %refs_4_.3, bf16[768,1536]{1,0:T(8,128)(2,1)} %collective-permute-done.1.refs_3_), custom_call_target="tpu_custom_call" | custom-call | bytes 15000 | tf_op jit(solution)/shard_map/up/pallas_call | solution.py:65
  36.3 2.3 %copy-done.1 = bf16[3072,768]{1,0:T(8,128)(2,1)S(1)} copy-done((bf16[3072,768]{1,0:T(8,128)(2,1)S(1)}, bf16[3072,768]{1,0:T(8,128)(2,1)}, u32[]{:S(2)}) %copy-start.1) | copy-done | bytes 4718616
  38.6 1.1 copy-done.10
  39.8 1.5 exchanged.3
  43.2 5.3 %all-to-all-start.3 = ((bf16[8,2,32,768]{3,2,1,0:T(8,128)(2,1)}), bf16[8,2,32,768]{3,2,1,0:T(8,128)(2,1)S(1)}, u32[]{:S(2)}, u32[]{:S(2)}) async-start(bf16[8,2,32,768]{3,2,1,0:T(8,128)(2,1)} %spread_kernel.5), calls=%async_computation.3 | async-start | bytes 1572864 | tf_op jit(solution)/shard_map/row_cot/all_to_all | solution.py:94
  48.5 6.8 %up.4.refs_1_ = bf16[4,2,64,1536]{3,2,1,0:T(8,128)(2,1)} custom-call(s32[1]{0:T(128)} %bitcast.core, bf16[8,2,32,768]{3,2,1,0:T(8,128)(2,1)} %copy-done.5, bf16[8,2,32,768]{3,2,1,0:T(8,128)(2,1)} %collective-permute-done.3.refs_1_, bf16[768,3072]{1,0:T(8,128)(2,1)} %refs_4_.3, bf16[768,1536]{1,0:T(8,128)(2,1)} %collective-permute-done.1.refs_3_), custom_call_target="tpu_custom_call" | custom-call | bytes 15000 | tf_op jit(solution)/shard_map/up/pallas_call | solution.py:65
  55.3 5.6 %all-to-all-done.3.refs_0_ = bf16[8,2,32,768]{3,2,1,0:T(8,128)(2,1)S(1)} async-done(((bf16[8,2,32,768]{3,2,1,0:T(8,128)(2,1)}), bf16[8,2,32,768]{3,2,1,0:T(8,128)(2,1)S(1)}, u32[]{:S(2)}, u32[]{:S(2)}) %all-to-all-start.3) | async-done | bytes 786464 | tf_op jit(solution)/shard_map/row_cot/all_to_all | solution.py:94
  60.9 5.3 %all-to-all-start.2 = ((bf16[4,2,64,1536]{3,2,1,0:T(8,128)(2,1)}), bf16[4,2,64,1536]{3,2,1,0:T(8,128)(2,1)}, u32[]{:S(2)}, u32[]{:S(2)}) async-start(bf16[4,2,64,1536]{3,2,1,0:T(8,128)(2,1)} %up.4.refs_1_), calls=%async_computation.2 | async-start | bytes 3145728 | tf_op jit(solution)/shard_map/sum_b_z/all_to_all | solution.py:366
  66.4 3.0 %collective-permute-start.2 = (bf16[256,1536]{1,0:T(8,128)(2,1)}, bf16[256,1536]{1,0:T(8,128)(2,1)S(1)}, u32[]{:S(2)}, u32[]{:S(2)}) collective-permute-start(bf16[256,1536]{1,0:T(8,128)(2,1)} %get-tuple-element.17), channel_id=1, source_target_pairs={{0,2},{2,0},{1,3},{3,1},{4,6},{6,4},{5,7},{7,5},{8,10},{10,8},{9,1... | collective-permute-start | bytes 2359304 | tf_op jit(solution)/shard_map/sum_a_y/ppermute | solution.py:38
  70.3 6.7 %up.5 = (bf16[256,1536]{1,0:T(8,128)(2,1)}, bf16[256,1536]{1,0:T(8,128)(2,1)}) custom-call(s32[1]{0:T(128)} %bitcast.core, bf16[8,2,32,768]{3,2,1,0:T(8,128)(2,1)} %copy-done.2, bf16[8,2,32,768]{3,2,1,0:T(8,128)(2,1)} %copy-done.22, bf16[3072,768]{1,0:T(8,128)(2,1)} %refs_4_.2, bf16[1536,768]{1,0:T(8,128)(2,1)} %collective-permute-done.5.refs_3_), custom_call_target="tpu_custom_call" | custom-call | bytes 15000 | tf_op jit(solution)/shard_map/up/pallas_call | solution.py:65
  77.1 8.9 %all-to-all-done.2.refs_0_ = bf16[4,2,64,1536]{3,2,1,0:T(8,128)(2,1)} async-done(((bf16[4,2,64,1536]{3,2,1,0:T(8,128)(2,1)}), bf16[4,2,64,1536]{3,2,1,0:T(8,128)(2,1)}, u32[]{:S(2)}, u32[]{:S(2)}) %all-to-all-start.2) | async-done | bytes 1572896 | tf_op jit(solution)/shard_map/sum_b_z/all_to_all | solution.py:366
  86.0 1.1 copy-done.16
  87.1 1.6 halves_of.1
  89.8 4.1 %all-to-all-start.4 = ((bf16[4,64,1536]{2,1,0:T(8,128)(2,1)}), bf16[4,64,1536]{2,1,0:T(8,128)(2,1)S(1)}, u32[]{:S(2)}, u32[]{:S(2)}) async-start(bf16[4,64,1536]{2,1,0:T(8,128)(2,1)} %bitcast.1), calls=%async_computation.4 | async-start | bytes 1572864 | tf_op jit(solution)/shard_map/sum_a_z/all_to_all | solution.py:366
  93.9 2.9 %collective-permute-start.6 = (bf16[64,1536]{1,0:T(8,128)(2,1)S(1)}, bf16[64,1536]{1,0:T(8,128)(2,1)S(1)}, u32[]{:S(2)}, u32[]{:S(2)}) collective-permute-start(bf16[64,1536]{1,0:T(8,128)(2,1)S(1)} %get-tuple-element.20), channel_id=1, source_target_pairs={{0,2},{2,0},{1,3},{3,1},{4,6},{6,4},{5,7},{7,5},{8,10},{10,8},{9,1... | collective-permute-start | bytes 589832 | tf_op jit(solution)/shard_map/sum_b_y/ppermute | solution.py:38
  97.5 5.4 %collective-permute-done.6.refs_1_ = bf16[64,1536]{1,0:T(8,128)(2,1)S(1)} collective-permute-done((bf16[64,1536]{1,0:T(8,128)(2,1)S(1)}, bf16[64,1536]{1,0:T(8,128)(2,1)S(1)}, u32[]{:S(2)}, u32[]{:S(2)}) %collective-permute-start.6) | collective-permute-done | bytes 196640 | tf_op jit(solution)/shard_map/sum_b_y/ppermute | solution.py:38
  103.1 2.9 %all-to-all-done.4.refs_0_ = bf16[4,64,1536]{2,1,0:T(8,128)(2,1)S(1)} async-done(((bf16[4,64,1536]{2,1,0:T(8,128)(2,1)}), bf16[4,64,1536]{2,1,0:T(8,128)(2,1)S(1)}, u32[]{:S(2)}, u32[]{:S(2)}) %all-to-all-start.4) | async-done | bytes 786464 | tf_op jit(solution)/shard_map/sum_a_z/all_to_all | solution.py:366
  107.1 4.2 %all-to-all-start.5 = ((bf16[4,64,1536]{2,1,0:T(8,128)(2,1)}), bf16[4,64,1536]{2,1,0:T(8,128)(2,1)}, u32[]{:S(2)}, u32[]{:S(2)}) async-start(bf16[4,64,1536]{2,1,0:T(8,128)(2,1)} %finish_a.1.refs_2_), calls=%async_computation.5 | async-start | bytes 1572864 | tf_op jit(solution)/shard_map/all_a_z/all_to_all | solution.py:366
  111.3 7.1 %collective-permute-done.10.refs_1_ = bf16[256,1536]{1,0:T(8,128)(2,1)S(1)} collective-permute-done((bf16[256,1536]{1,0:T(8,128)(2,1)}, bf16[256,1536]{1,0:T(8,128)(2,1)S(1)}, u32[]{:S(2)}, u32[]{:S(2)}) %collective-permute-start.10) | collective-permute-done | bytes 786464 | tf_op jit(solution)/shard_map/sum_cot_y/ppermute | solution.py:38
  119.5 3.0 %all-to-all-done.5 = bf16[4,64,1536]{2,1,0:T(8,128)(2,1)} async-done(((bf16[4,64,1536]{2,1,0:T(8,128)(2,1)}), bf16[4,64,1536]{2,1,0:T(8,128)(2,1)}, u32[]{:S(2)}, u32[]{:S(2)}) %all-to-all-start.5) | async-done | bytes 786464 | tf_op jit(solution)/shard_map/all_a_z/all_to_all | solution.py:366
  122.5 3.5 %all-to-all-start.6 = ((bf16[4,64,1536]{2,1,0:T(8,128)(2,1)}), bf16[4,64,1536]{2,1,0:T(8,128)(2,1)S(1)}, u32[]{:S(2)}, u32[]{:S(2)}) async-start(bf16[4,64,1536]{2,1,0:T(8,128)(2,1)} %bitcast.3), calls=%async_computation.6 | async-start | bytes 1572864 | tf_op jit(solution)/shard_map/sum_cot_z/all_to_all | solution.py:366
  126.0 3.0 %collective-permute-start.7 = (bf16[256,1536]{1,0:T(8,128)(2,1)}, bf16[256,1536]{1,0:T(8,128)(2,1)}, u32[]{:S(2)}, u32[]{:S(2)}) collective-permute-start(bf16[256,1536]{1,0:T(8,128)(2,1)} %bitcast.2.refs_0_), channel_id=1, source_target_pairs={{0,2},{2,0},{1,3},{3,1},{4,6},{6,4},{5,7},{7,5},{8,10},{10,8},{9,1... | collective-permute-start | bytes 2359304 | tf_op jit(solution)/shard_map/all_a_y/ppermute | solution.py:38
  129.0 6.9 %all-to-all-done.6.refs_0_ = bf16[4,64,1536]{2,1,0:T(8,128)(2,1)S(1)} async-done(((bf16[4,64,1536]{2,1,0:T(8,128)(2,1)}), bf16[4,64,1536]{2,1,0:T(8,128)(2,1)S(1)}, u32[]{:S(2)}, u32[]{:S(2)}) %all-to-all-start.6) | async-done | bytes 786464 | tf_op jit(solution)/shard_map/sum_cot_z/all_to_all | solution.py:366
  135.9 1.2 finish_back.1.refs_5_
  137.2 4.2 %all-to-all-start.8 = ((bf16[4,64,1536]{2,1,0:T(8,128)(2,1)}), bf16[4,64,1536]{2,1,0:T(8,128)(2,1)}, u32[]{:S(2)}, u32[]{:S(2)}) async-start(bf16[4,64,1536]{2,1,0:T(8,128)(2,1)} %finish_back.1.refs_5_), calls=%async_computation.8 | async-start | bytes 1572864 | tf_op jit(solution)/shard_map/all_back_z/all_to_all | solution.py:366
  141.4 3.0 %collective-permute-start.14 = (bf16[64,1536]{1,0:T(8,128)(2,1)S(1)}, bf16[64,1536]{1,0:T(8,128)(2,1)S(1)}, u32[]{:S(2)}, u32[]{:S(2)}) collective-permute-start(bf16[64,1536]{1,0:T(8,128)(2,1)S(1)} %get-tuple-element.23.refs_0_), channel_id=1, source_target_pairs={{0,2},{2,0},{1,3},{3,1},{4,6},{6,4},{5,7},{7,5},{8,10},{10,8},{9,1... | collective-permute-start | bytes 589832 | tf_op jit(solution)/shard_map/all_b_y/ppermute | solution.py:38
  144.3 4.4 %collective-permute-done.14.refs_1_ = bf16[64,1536]{1,0:T(8,128)(2,1)S(1)} collective-permute-done((bf16[64,1536]{1,0:T(8,128)(2,1)S(1)}, bf16[64,1536]{1,0:T(8,128)(2,1)S(1)}, u32[]{:S(2)}, u32[]{:S(2)}) %collective-permute-start.14) | collective-permute-done | bytes 196640 | tf_op jit(solution)/shard_map/all_b_y/ppermute | solution.py:38
  148.7 2.2 all-to-all-done.8
  151.0 1.1 copy-done.15
  152.2 3.6 %all-to-all-start.9 = ((bf16[4,2,64,1536]{3,2,1,0:T(8,128)(2,1)}), bf16[4,2,64,1536]{3,2,1,0:T(8,128)(2,1)S(1)}, u32[]{:S(2)}, u32[]{:S(2)}) async-start(bf16[4,2,64,1536]{3,2,1,0:T(8,128)(2,1)} %copy-done.15), calls=%async_computation.9 | async-start | bytes 3145728 | tf_op jit(solution)/shard_map/all_b_z/all_to_all | solution.py:366
  156.3 2.9 %collective-permute-start.11 = (bf16[256,1536]{1,0:T(8,128)(2,1)}, bf16[256,1536]{1,0:T(8,128)(2,1)S(1)}, u32[]{:S(2)}, u32[]{:S(2)}) collective-permute-start(bf16[256,1536]{1,0:T(8,128)(2,1)} %bitcast.5.refs_3_.refs_0_.refs_1_), channel_id=1, source_target_pairs={{0,2},{2,0},{1,3},{3,1},{4,6},{6,4},{5,7},{7,5},{8,10},{10,8},{9,1... | collective-permute-start | bytes 2359304 | tf_op jit(solution)/shard_map/all_back_y/ppermute | solution.py:38
  159.6 7.1 %down.2.refs_1_.refs_3_ = bf16[8,2,32,768]{3,2,1,0:T(8,128)(2,1)} custom-call(s32[1]{0:T(128)} %bitcast.core, bf16[256,1536]{1,0:T(8,128)(2,1)} %bitcast.2.refs_0_, bf16[256,1536]{1,0:T(8,128)(2,1)} %collective-permute-done.7.refs_1_.refs_2_, bf16[256,1536]{1,0:T(8,128)(2,1)} %collective-permute-done.8.refs_2_, ...), custom_call_target="tpu_custom_call" | custom-call | bytes 18000 | tf_op jit(solution)/shard_map/down/pallas_call | solution.py:65
  166.7 10.9 %collective-permute-done.11.refs_0_.refs_2_.refs_1_ = bf16[256,1536]{1,0:T(8,128)(2,1)S(1)} collective-permute-done((bf16[256,1536]{1,0:T(8,128)(2,1)}, bf16[256,1536]{1,0:T(8,128)(2,1)S(1)}, u32[]{:S(2)}, u32[]{:S(2)}) %collective-permute-start.11) | collective-permute-done | bytes 786464 | tf_op jit(solution)/shard_map/all_back_y/ppermute | solution.py:38
  177.6 1.2 relay.7
  180.2 1.1 copy-done.8
  182.4 4.2 %all-to-all-start.7 = ((bf16[8,2,32,768]{3,2,1,0:T(8,128)(2,1)}), bf16[8,2,32,768]{3,2,1,0:T(8,128)(2,1)}, u32[]{:S(2)}, u32[]{:S(2)}) async-start(bf16[8,2,32,768]{3,2,1,0:T(8,128)(2,1)} %down.2.refs_1_.refs_3_), calls=%async_computation.7 | async-start | bytes 1572864 | tf_op jit(solution)/shard_map/row_out/all_to_all | solution.py:120
  186.6 6.3 %grad.2.refs_5_ = bf16[3072,768]{1,0:T(8,128)(2,1)} custom-call(s32[1]{0:T(128)} %bitcast.core, bf16[8,2,32,768]{3,2,1,0:T(8,128)(2,1)S(1)} %copy-done.3, bf16[4,2,64,1536]{3,2,1,0:T(8,128)(2,1)S(1)} %all-to-all-done.9.refs_0_.refs_1_, bf16[4,2,64,1536]{3,2,1,0:T(8,128)(2,1)} %collective-permute-done.15.refs_2_, bf16[8,2,32,768]{3,2,1,0:T(8,128)(2,1)} %down.2.refs_1_.refs_3_), custom_call_target="tpu_custom_call" | custom-call | bytes 18000 | tf_op jit(solution)/shard_map/grad/pallas_call | solution.py:65
  193.0 7.2 %down.3.refs_5_ = bf16[8,2,32,768]{3,2,1,0:T(8,128)(2,1)} custom-call(s32[1]{0:T(128)} %bitcast.core, bf16[256,1536]{1,0:T(8,128)(2,1)} %bitcast.5.refs_3_.refs_0_.refs_1_, bf16[256,1536]{1,0:T(8,128)(2,1)} %copy-done.7, bf16[256,1536]{1,0:T(8,128)(2,1)} %collective-permute-done.12.refs_2_.refs_3_, ...), custom_call_target="tpu_custom_call" | custom-call | bytes 18000 | tf_op jit(solution)/shard_map/down/pallas_call | solution.py:65
  200.8 5.1 %all-to-all-start.10 = ((bf16[8,2,32,768]{3,2,1,0:T(8,128)(2,1)}), bf16[8,2,32,768]{3,2,1,0:T(8,128)(2,1)}, u32[]{:S(2)}, u32[]{:S(2)}) async-start(bf16[8,2,32,768]{3,2,1,0:T(8,128)(2,1)} %down.3.refs_5_), calls=%async_computation.10 | async-start | bytes 1572864 | tf_op jit(solution)/shard_map/row_in/all_to_all | solution.py:120
  206.7 1.9 settle_kernel.2
  208.6 1.1 copy-done.14
  209.7 6.4 %grad.3 = (bf16[768,3072]{1,0:T(8,128)(2,1)}, f32[1,3072]{1,0:T(1,128)}) custom-call(s32[1]{0:T(128)} %bitcast.core, bf16[8,2,32,768]{3,2,1,0:T(8,128)(2,1)S(1)} %copy-done.6, bf16[256,1536]{1,0:T(8,128)(2,1)} %bitcast.5.refs_3_.refs_0_.refs_1_, bf16[256,1536]{1,0:T(8,128)(2,1)S(1)} %copy-done.9, bf16[256,1536]{1,0:T(8,128)(2,1)} %collective-permute-done.12.refs_2_.refs_3_, ...), custom_call_target="tpu_custom_call" | custom-call | bytes 18000 | tf_op jit(solution)/shard_map/grad/pallas_call | solution.py:65
  216.1 2.8 %all-to-all-done.10 = bf16[8,2,32,768]{3,2,1,0:T(8,128)(2,1)} async-done(((bf16[8,2,32,768]{3,2,1,0:T(8,128)(2,1)}), bf16[8,2,32,768]{3,2,1,0:T(8,128)(2,1)}, u32[]{:S(2)}, u32[]{:S(2)}) %all-to-all-start.10) | async-done | bytes 786464 | tf_op jit(solution)/shard_map/row_in/all_to_all | solution.py:120
  218.9 1.9 settle_kernel.3
  (85 shorter events, 15.6 us)
Async XLA Ops:
  19.3 2.3 %copy-start = (bf16[768,3072]{1,0:T(8,128)(2,1)S(1)}, bf16[768,3072]{1,0:T(8,128)(2,1)}, u32[]{:S(2)}) copy-start(bf16[768,3072]{1,0:T(8,128)(2,1)} %refs_4_.3) | copy-start | bytes 14155780
  21.7 1.7 copy-start.13
  21.7 2.2 %copy-start.19 = (bf16[64,768]{1,0:T(8,128)(2,1)S(1)}, bf16[64,768]{1,0:T(8,128)(2,1)}, u32[]{:S(2)}) copy-start(bf16[64,768]{1,0:T(8,128)(2,1)} %refs_0_.7) | copy-start | bytes 294916
  23.4 6.0 %collective-permute-start.1 = (bf16[768,1536]{1,0:T(8,128)(2,1)}, bf16[768,1536]{1,0:T(8,128)(2,1)}, u32[]{:S(2)}, u32[]{:S(2)}) collective-permute-start(bf16[768,1536]{1,0:T(8,128)(2,1)} %exchanged.2), channel_id=1, source_target_pairs={{0,1},{1,0},{2,3},{3,2},{4,5},{5,4},{6,7},{7,6},{8,9},{9,8},{10,11... | collective-permute-start | bytes 7077896 | tf_op jit(solution)/shard_map/core_swap/ppermute | solution.py:38
  23.4 5.3 %collective-permute-start = (bf16[8,2,32,768]{3,2,1,0:T(8,128)(2,1)S(1)}, bf16[8,2,32,768]{3,2,1,0:T(8,128)(2,1)S(1)}, u32[]{:S(2)}, u32[]{:S(2)}) collective-permute-start(bf16[8,2,32,768]{3,2,1,0:T(8,128)(2,1)S(1)} %all_to_all.55.refs_1_.refs_0_), channel_id=1, source_target_pairs={{0,1},{1,0},{2,3},{3,2},{4,5},{5,4},{6,7},{7,6},{8,9},{9,8},{10,11... | collective-permute-start | bytes 2359304 | tf_op jit(solution)/shard_map/core_swap/ppermute | solution.py:38
  24.8 16.8 %all-to-all-start.1 = ((bf16[8,2,32,768]{3,2,1,0:T(8,128)(2,1)}), bf16[8,2,32,768]{3,2,1,0:T(8,128)(2,1)S(1)}, u32[]{:S(2)}, u32[]{:S(2)}) async-start(bf16[8,2,32,768]{3,2,1,0:T(8,128)(2,1)} %spread_kernel.4), calls=%async_computation.1 | async-start | bytes 1572864 | tf_op jit(solution)/shard_map/row_b/all_to_all | solution.py:94
  28.7 0.9 copy-start.21
  36.3 2.3 %copy-start.1 = (bf16[3072,768]{1,0:T(8,128)(2,1)S(1)}, bf16[3072,768]{1,0:T(8,128)(2,1)}, u32[]{:S(2)}) copy-start(bf16[3072,768]{1,0:T(8,128)(2,1)} %refs_4_.2) | copy-start | bytes 14155780
  38.6 1.1 copy-start.10
  39.8 1.9 copy-start.11
  41.2 28.1 %collective-permute-start.5 = (bf16[1536,768]{1,0:T(8,128)(2,1)}, bf16[1536,768]{1,0:T(8,128)(2,1)}, u32[]{:S(2)}, u32[]{:S(2)}) collective-permute-start(bf16[1536,768]{1,0:T(8,128)(2,1)} %exchanged.3), channel_id=1, source_target_pairs={{0,1},{1,0},{2,3},{3,2},{4,5},{5,4},{6,7},{7,6},{8,9},{9,8},{10,11... | collective-permute-start | bytes 7077896 | tf_op jit(solution)/shard_map/core_swap/ppermute | solution.py:38
  41.6 1.5 copy-start.5
  41.7 6.8 %collective-permute-start.3 = (bf16[8,2,32,768]{3,2,1,0:T(8,128)(2,1)S(1)}, bf16[8,2,32,768]{3,2,1,0:T(8,128)(2,1)}, u32[]{:S(2)}, u32[]{:S(2)}) collective-permute-start(bf16[8,2,32,768]{3,2,1,0:T(8,128)(2,1)S(1)} %relay.4), channel_id=1, source_target_pairs={{0,1},{1,0},{2,3},{3,2},{4,5},{5,4},{6,7},{7,6},{8,9},{9,8},{10,11... | collective-permute-start | bytes 2359304 | tf_op jit(solution)/shard_map/core_swap/ppermute | solution.py:38
  43.2 17.7 %all-to-all-start.3 = ((bf16[8,2,32,768]{3,2,1,0:T(8,128)(2,1)}), bf16[8,2,32,768]{3,2,1,0:T(8,128)(2,1)S(1)}, u32[]{:S(2)}, u32[]{:S(2)}) async-start(bf16[8,2,32,768]{3,2,1,0:T(8,128)(2,1)} %spread_kernel.5), calls=%async_computation.3 | async-start | bytes 1572864 | tf_op jit(solution)/shard_map/row_cot/all_to_all | solution.py:94
  55.3 10.9 %copy-start.4 = (bf16[4,2,64,1536]{3,2,1,0:T(8,128)(2,1)S(1)}, bf16[4,2,64,1536]{3,2,1,0:T(8,128)(2,1)}, u32[]{:S(2)}) copy-start(bf16[4,2,64,1536]{3,2,1,0:T(8,128)(2,1)} %up.4.refs_1_) | copy-start | bytes 4718596
  60.9 5.4 %copy-start.2 = (bf16[8,2,32,768]{3,2,1,0:T(8,128)(2,1)}, bf16[8,2,32,768]{3,2,1,0:T(8,128)(2,1)S(1)}, u32[]{:S(2)}) copy-start(bf16[8,2,32,768]{3,2,1,0:T(8,128)(2,1)S(1)} %all-to-all-done.3.refs_0_) | copy-start | bytes 2359300
  60.9 25.1 %all-to-all-start.2 = ((bf16[4,2,64,1536]{3,2,1,0:T(8,128)(2,1)}), bf16[4,2,64,1536]{3,2,1,0:T(8,128)(2,1)}, u32[]{:S(2)}, u32[]{:S(2)}) async-start(bf16[4,2,64,1536]{3,2,1,0:T(8,128)(2,1)} %up.4.refs_1_), calls=%async_computation.2 | async-start | bytes 3145728 | tf_op jit(solution)/shard_map/sum_b_z/all_to_all | solution.py:366
  66.3 3.1 %collective-permute-start.4 = (bf16[8,2,32,768]{3,2,1,0:T(8,128)(2,1)S(1)}, bf16[8,2,32,768]{3,2,1,0:T(8,128)(2,1)S(1)}, u32[]{:S(2)}, u32[]{:S(2)}) collective-permute-start(bf16[8,2,32,768]{3,2,1,0:T(8,128)(2,1)S(1)} %relay.5), channel_id=1, source_target_pairs={{0,1},{1,0},{2,3},{3,2},{4,5},{5,4},{6,7},{7,6},{8,9},{9,8},{10,11... | collective-permute-start | bytes 2359304 | tf_op jit(solution)/shard_map/core_swap/ppermute | solution.py:38
  66.4 22.4 %collective-permute-start.2 = (bf16[256,1536]{1,0:T(8,128)(2,1)}, bf16[256,1536]{1,0:T(8,128)(2,1)S(1)}, u32[]{:S(2)}, u32[]{:S(2)}) collective-permute-start(bf16[256,1536]{1,0:T(8,128)(2,1)} %get-tuple-element.17), channel_id=1, source_target_pairs={{0,2},{2,0},{1,3},{3,1},{4,6},{6,4},{5,7},{7,5},{8,10},{10,8},{9,1... | collective-permute-start | bytes 2359304 | tf_op jit(solution)/shard_map/sum_a_y/ppermute | solution.py:38
  69.3 1.0 copy-start.22
  77.1 11.7 %copy-start.12 = (bf16[256,1536]{1,0:T(8,128)(2,1)S(1)}, bf16[256,1536]{1,0:T(8,128)(2,1)}, u32[]{:S(2)}) copy-start(bf16[256,1536]{1,0:T(8,128)(2,1)} %get-tuple-element.16.refs_1_.refs_0_) | copy-start | bytes 2359300
  86.0 1.1 copy-start.16
  88.7 8.7 %copy-start.23 = (f32[3072]{0:T(1024)S(1)}, f32[3072]{0:T(1024)}, u32[]{:S(2)}) copy-start(f32[3072]{0:T(1024)} %param.11) | copy-start | bytes 36868
  89.8 16.2 %all-to-all-start.4 = ((bf16[4,64,1536]{2,1,0:T(8,128)(2,1)}), bf16[4,64,1536]{2,1,0:T(8,128)(2,1)S(1)}, u32[]{:S(2)}, u32[]{:S(2)}) async-start(bf16[4,64,1536]{2,1,0:T(8,128)(2,1)} %bitcast.1), calls=%async_computation.4 | async-start | bytes 1572864 | tf_op jit(solution)/shard_map/sum_a_z/all_to_all | solution.py:366
  93.9 24.5 %copy-start.17 = (bf16[256,1536]{1,0:T(8,128)(2,1)S(1)}, bf16[256,1536]{1,0:T(8,128)(2,1)}, u32[]{:S(2)}) copy-start(bf16[256,1536]{1,0:T(8,128)(2,1)} %get-tuple-element.18.refs_1_.refs_0_) | copy-start | bytes 2359300
  93.9 9.0 %collective-permute-start.6 = (bf16[64,1536]{1,0:T(8,128)(2,1)S(1)}, bf16[64,1536]{1,0:T(8,128)(2,1)S(1)}, u32[]{:S(2)}, u32[]{:S(2)}) collective-permute-start(bf16[64,1536]{1,0:T(8,128)(2,1)S(1)} %get-tuple-element.20), channel_id=1, source_target_pairs={{0,2},{2,0},{1,3},{3,1},{4,6},{6,4},{5,7},{7,5},{8,10},{10,8},{9,1... | collective-permute-start | bytes 589832 | tf_op jit(solution)/shard_map/sum_b_y/ppermute | solution.py:38
  96.8 21.6 %collective-permute-start.10 = (bf16[256,1536]{1,0:T(8,128)(2,1)}, bf16[256,1536]{1,0:T(8,128)(2,1)S(1)}, u32[]{:S(2)}, u32[]{:S(2)}) collective-permute-start(bf16[256,1536]{1,0:T(8,128)(2,1)} %get-tuple-element.22), channel_id=1, source_target_pairs={{0,2},{2,0},{1,3},{3,1},{4,6},{6,4},{5,7},{7,5},{8,10},{10,8},{9,1... | collective-permute-start | bytes 2359304 | tf_op jit(solution)/shard_map/sum_cot_y/ppermute | solution.py:38
  107.1 15.4 %all-to-all-start.5 = ((bf16[4,64,1536]{2,1,0:T(8,128)(2,1)}), bf16[4,64,1536]{2,1,0:T(8,128)(2,1)}, u32[]{:S(2)}, u32[]{:S(2)}) async-start(bf16[4,64,1536]{2,1,0:T(8,128)(2,1)} %finish_a.1.refs_2_), calls=%async_computation.5 | async-start | bytes 1572864 | tf_op jit(solution)/shard_map/all_a_z/all_to_all | solution.py:366
  122.5 13.4 %all-to-all-start.6 = ((bf16[4,64,1536]{2,1,0:T(8,128)(2,1)}), bf16[4,64,1536]{2,1,0:T(8,128)(2,1)S(1)}, u32[]{:S(2)}, u32[]{:S(2)}) async-start(bf16[4,64,1536]{2,1,0:T(8,128)(2,1)} %bitcast.3), calls=%async_computation.6 | async-start | bytes 1572864 | tf_op jit(solution)/shard_map/sum_cot_z/all_to_all | solution.py:366
  126.0 22.7 %collective-permute-start.7 = (bf16[256,1536]{1,0:T(8,128)(2,1)}, bf16[256,1536]{1,0:T(8,128)(2,1)}, u32[]{:S(2)}, u32[]{:S(2)}) collective-permute-start(bf16[256,1536]{1,0:T(8,128)(2,1)} %bitcast.2.refs_0_), channel_id=1, source_target_pairs={{0,2},{2,0},{1,3},{3,1},{4,6},{6,4},{5,7},{7,5},{8,10},{10,8},{9,1... | collective-permute-start | bytes 2359304 | tf_op jit(solution)/shard_map/all_a_y/ppermute | solution.py:38
  137.2 13.7 %all-to-all-start.8 = ((bf16[4,64,1536]{2,1,0:T(8,128)(2,1)}), bf16[4,64,1536]{2,1,0:T(8,128)(2,1)}, u32[]{:S(2)}, u32[]{:S(2)}) async-start(bf16[4,64,1536]{2,1,0:T(8,128)(2,1)} %finish_back.1.refs_5_), calls=%async_computation.8 | async-start | bytes 1572864 | tf_op jit(solution)/shard_map/all_back_z/all_to_all | solution.py:366
  141.4 7.3 %collective-permute-start.14 = (bf16[64,1536]{1,0:T(8,128)(2,1)S(1)}, bf16[64,1536]{1,0:T(8,128)(2,1)S(1)}, u32[]{:S(2)}, u32[]{:S(2)}) collective-permute-start(bf16[64,1536]{1,0:T(8,128)(2,1)S(1)} %get-tuple-element.23.refs_0_), channel_id=1, source_target_pairs={{0,2},{2,0},{1,3},{3,1},{4,6},{6,4},{5,7},{7,5},{8,10},{10,8},{9,1... | collective-permute-start | bytes 589832 | tf_op jit(solution)/shard_map/all_b_y/ppermute | solution.py:38
  151.0 1.1 copy-start.15
  152.2 25.4 %all-to-all-start.9 = ((bf16[4,2,64,1536]{3,2,1,0:T(8,128)(2,1)}), bf16[4,2,64,1536]{3,2,1,0:T(8,128)(2,1)S(1)}, u32[]{:S(2)}, u32[]{:S(2)}) async-start(bf16[4,2,64,1536]{3,2,1,0:T(8,128)(2,1)} %copy-done.15), calls=%async_computation.9 | async-start | bytes 3145728 | tf_op jit(solution)/shard_map/all_b_z/all_to_all | solution.py:366
  155.7 3.5 %collective-permute-start.8 = (bf16[256,1536]{1,0:T(8,128)(2,1)}, bf16[256,1536]{1,0:T(8,128)(2,1)}, u32[]{:S(2)}, u32[]{:S(2)}) collective-permute-start(bf16[256,1536]{1,0:T(8,128)(2,1)} %bitcast.2.refs_0_), channel_id=1, source_target_pairs={{0,1},{1,0},{2,3},{3,2},{4,5},{5,4},{6,7},{7,6},{8,9},{9,8},{10,11... | collective-permute-start | bytes 2359304 | tf_op jit(solution)/shard_map/core_swap/ppermute | solution.py:38
  155.8 3.7 %collective-permute-start.9 = (bf16[256,1536]{1,0:T(8,128)(2,1)}, bf16[256,1536]{1,0:T(8,128)(2,1)}, u32[]{:S(2)}, u32[]{:S(2)}) collective-permute-start(bf16[256,1536]{1,0:T(8,128)(2,1)} %collective-permute-done.7.refs_1_.refs_2_), channel_id=1, source_target_pairs={{0,1},{1,0},{2,3},{3,2},{4,5},{5,4},{6,7},{7,6},{8,9},{9,8},{10,11... | collective-permute-start | bytes 2359304 | tf_op jit(solution)/shard_map/core_swap/ppermute | solution.py:38
  156.3 21.3 %collective-permute-start.11 = (bf16[256,1536]{1,0:T(8,128)(2,1)}, bf16[256,1536]{1,0:T(8,128)(2,1)S(1)}, u32[]{:S(2)}, u32[]{:S(2)}) collective-permute-start(bf16[256,1536]{1,0:T(8,128)(2,1)} %bitcast.5.refs_3_.refs_0_.refs_1_), channel_id=1, source_target_pairs={{0,2},{2,0},{1,3},{3,1},{4,6},{6,4},{5,7},{7,5},{8,10},{10,8},{9,1... | collective-permute-start | bytes 2359304 | tf_op jit(solution)/shard_map/all_back_y/ppermute | solution.py:38
  179.7 6.9 %copy-start.3 = (bf16[8,2,32,768]{3,2,1,0:T(8,128)(2,1)S(1)}, bf16[8,2,32,768]{3,2,1,0:T(8,128)(2,1)}, u32[]{:S(2)}) copy-start(bf16[8,2,32,768]{3,2,1,0:T(8,128)(2,1)} %copy-done.2) | copy-start | bytes 2359300
  179.7 6.9 %collective-permute-start.15 = (bf16[4,2,64,1536]{3,2,1,0:T(8,128)(2,1)}, bf16[4,2,64,1536]{3,2,1,0:T(8,128)(2,1)}, u32[]{:S(2)}, u32[]{:S(2)}) collective-permute-start(bf16[4,2,64,1536]{3,2,1,0:T(8,128)(2,1)} %relay.7), channel_id=1, source_target_pairs={{0,1},{1,0},{2,3},{3,2},{4,5},{5,4},{6,7},{7,6},{8,9},{9,8},{10,11... | collective-permute-start | bytes 4718600 | tf_op jit(solution)/shard_map/core_swap/ppermute | solution.py:38
  179.7 13.2 %collective-permute-start.12 = (bf16[256,1536]{1,0:T(8,128)(2,1)}, bf16[256,1536]{1,0:T(8,128)(2,1)}, u32[]{:S(2)}, u32[]{:S(2)}) collective-permute-start(bf16[256,1536]{1,0:T(8,128)(2,1)} %bitcast.5.refs_3_.refs_0_.refs_1_), channel_id=1, source_target_pairs={{0,1},{1,0},{2,3},{3,2},{4,5},{5,4},{6,7},{7,6},{8,9},{9,8},{10,11... | collective-permute-start | bytes 2359304 | tf_op jit(solution)/shard_map/core_swap/ppermute | solution.py:38
  180.2 1.1 copy-start.8
  182.4 10.6 %collective-permute-start.13 = (bf16[256,1536]{1,0:T(8,128)(2,1)}, bf16[256,1536]{1,0:T(8,128)(2,1)}, u32[]{:S(2)}, u32[]{:S(2)}) collective-permute-start(bf16[256,1536]{1,0:T(8,128)(2,1)} %relay.6), channel_id=1, source_target_pairs={{0,1},{1,0},{2,3},{3,2},{4,5},{5,4},{6,7},{7,6},{8,9},{9,8},{10,11... | collective-permute-start | bytes 2359304 | tf_op jit(solution)/shard_map/core_swap/ppermute | solution.py:38
  182.4 18.5 %all-to-all-start.7 = ((bf16[8,2,32,768]{3,2,1,0:T(8,128)(2,1)}), bf16[8,2,32,768]{3,2,1,0:T(8,128)(2,1)}, u32[]{:S(2)}, u32[]{:S(2)}) async-start(bf16[8,2,32,768]{3,2,1,0:T(8,128)(2,1)} %down.2.refs_1_.refs_3_), calls=%async_computation.7 | async-start | bytes 1572864 | tf_op jit(solution)/shard_map/row_out/all_to_all | solution.py:120
  192.9 13.0 %copy-start.24 = (f32[768]{0:T(1024)S(1)}, f32[768]{0:T(1024)}, u32[]{:S(2)}) copy-start(f32[768]{0:T(1024)} %param.13) | copy-start | bytes 9220
  200.2 8.4 %copy-start.6 = (bf16[8,2,32,768]{3,2,1,0:T(8,128)(2,1)S(1)}, bf16[8,2,32,768]{3,2,1,0:T(8,128)(2,1)}, u32[]{:S(2)}) copy-start(bf16[8,2,32,768]{3,2,1,0:T(8,128)(2,1)} %copy-done.5) | copy-start | bytes 2359300
  200.2 8.4 %copy-start.9 = (bf16[256,1536]{1,0:T(8,128)(2,1)S(1)}, bf16[256,1536]{1,0:T(8,128)(2,1)}, u32[]{:S(2)}) copy-start(bf16[256,1536]{1,0:T(8,128)(2,1)} %copy-done.7) | copy-start | bytes 2359300
  200.8 18.1 %all-to-all-start.10 = ((bf16[8,2,32,768]{3,2,1,0:T(8,128)(2,1)}), bf16[8,2,32,768]{3,2,1,0:T(8,128)(2,1)}, u32[]{:S(2)}, u32[]{:S(2)}) async-start(bf16[8,2,32,768]{3,2,1,0:T(8,128)(2,1)} %down.3.refs_5_), calls=%async_computation.10 | async-start | bytes 1572864 | tf_op jit(solution)/shard_map/row_in/all_to_all | solution.py:120
  208.6 1.1 copy-start.14
  (3 other events, 2.7 us)
